TPU v7x, 32 devices: a whole 2x2x4 slice. The times are simulated.
32 devices in a mesh: gx: 4 (over y, core), gy: 8 (over z, x).
Axes of the slice: x: 2, y: 2, z: 4, core: 2. Of those that a mesh axis runs over, the one named last changes fastest.
Arguments:
- inputs: bfloat16 [2, 128, 64, 768], P(None, ('gx', 'gy')), may hold values from -6 to 6
- lengths: int32 [2, 128], P(None, ('gx', 'gy')), may hold values from 3 to 64, as said below
- labels: int32 [128], P(('gx', 'gy')), may hold values from 0 to 127, as said below
- attention_input_weight: bfloat16 [2, 768, 2304], replicated, may hold values from -0.21875 to 0.21875
- attention_output_matrix: bfloat16 [2, 768, 768], replicated, may hold values from -0.875 to 0.875
- widen_weight: bfloat16 [2, 768, 3072], replicated, may hold values from -0.21875 to 0.21875
- narrowing_weight: bfloat16 [2, 3072, 768], replicated, may hold values from -0.109375 to 0.109375
- layer_bias_rows: float32 [2, 6, 768], replicated, may hold values from -1 to 1
- norm_gains: float32 [2, 2, 768], replicated, may hold values from 0.5 to 1.5
- widen_bias: float32 [2, 3072], replicated, may hold values from -1 to 1
- pool_weight: bfloat16 [768, 768], replicated, may hold values from -0.21875 to 0.21875
- pool_bias: float32 [768], replicated, may hold values from -1 to 1
Outputs:
- row_loss: float32 [128], P(('gx', 'gy'))
- input_grad: float32 [2, 128, 64, 768], P(None, ('gx', 'gy'))
- scaled_grad: float32 [2, 128, 64, 768], P(None, ('gx', 'gy'))
- grad_attend: float32 [2, 768, 2304], P(None, 'gx', 'gy')
- grad_output: float32 [2, 768, 768], P(None, 'gx', 'gy')
- grad_expand: float32 [2, 768, 3072], P(None, 'gx', 'gy')
- grad_reduce: float32 [2, 3072, 768], P(None, 'gx', 'gy')
- grad_bias_rows: float32 [2, 6, 768], P(None, None, ('gx', 'gy'))
- grad_gains: float32 [2, 2, 768], P(None, None, ('gx', 'gy'))
- grad_expand_bias: float32 [2, 3072], P(None, ('gx', 'gy'))
- grad_pool: float32 [768, 768], P('gx', 'gy')
- grad_pool_bias: float32 [768], P(('gx', 'gy'))
Inputs may be any that keep to these rules, and one draw needn't show every extreme that they name: `lengths`: real tokens of each sentence; later positions are padding. `labels`: every target is the positive of exactly one source.
All inputs are finite; a program needn't handle non-finite values.
Results may differ from a plain program's by a relative error of at most 0.025.
Values may be sent and summed in bfloat16 or wider, within the bound.
No kernel may reach another device: no remote copies, remote signals or barrier semaphores. Data moves between devices by JAX's collectives and lax.ppermute only.
A program may use at most 320 MiB of HBM per device.

v0:
```python
import functools
import jax
import jax.numpy as jnp
from jax import lax
from jax.sharding import PartitionSpec as P
from jax.experimental import pallas as pl
from jax.experimental.pallas import tpu as pltpu

H = 12
HD = 64


class Cut:
    def __init__(self, C, Y, X, Z):
        self.C, self.Y, self.X, self.Z = C, Y, X, Z
        self.GX, self.GY = C * Y, X * Z


BF = jnp.bfloat16
F32 = jnp.float32
ROOT_HALF = 0.7071067811865476
PHI_ZERO = 0.3989422804014327
MASKED = -1e9
EPS_NORM = 1e-12
EPS_UNIT = 1e-6
SCORE = 10.0
MARGIN = 0.3
SCALE = HD ** -0.5

NN = (((1,), (0,)), ((), ()))
NT = (((1,), (1,)), ((), ()))
TN = (((0,), (0,)), ((), ()))


def place():
    gx, gy = lax.axis_index("gx"), lax.axis_index("gy")
    return gx, lax.rem(gx, 2), lax.div(gx, 2), lax.rem(gy, 2), lax.div(gy, 2), gy


def dot(a, b, dims=NN):
    return lax.dot_general(a, b, dims, preferred_element_type=F32)


def normalize(z):
    centered = z - jnp.mean(z, -1, keepdims=True)
    variance = jnp.mean(centered * centered, -1, keepdims=True)
    root = lax.rsqrt(variance + EPS_NORM)
    return centered * root, root


def gelu_pair(f):
    cdf = 0.5 * (1.0 + lax.erf(f * ROOT_HALF))
    return f * cdf, cdf + f * (PHI_ZERO * jnp.exp(-0.5 * f * f))


def head_rows(values):
    lanes = lax.broadcasted_iota(jnp.int32, values.shape, 1) // HD
    return jnp.concatenate([jnp.where(lanes == h, values, 0) for h in range(H)], 0)


def head_fold(values):
    r = values.shape[0] // H
    lanes = lax.broadcasted_iota(jnp.int32, (r, values.shape[1]), 1) // HD
    out = jnp.zeros((r, values.shape[1]), values.dtype)
    for h in range(H):
        out = jnp.where(lanes == h, values[h * r:(h + 1) * r], out)
    return out


def by_core(cut, src, act, slot):
    if cut.C == 1:
        act[0, slot] = src[...]
        return
    width = src.shape[1] // cut.GX
    for ci in range(2):
        act[ci, slot] = jnp.concatenate(
            [src[:, (2 * y + ci) * width:(2 * y + ci + 1) * width] for y in range(cut.Y)], 1)


def fwd_kernel(cut, len_ref, lab_ref, x_hbm, wqkv_hbm, wo_hbm, w1_hbm, w2_hbm, wp_hbm, bias_ref, gain_ref, wb_ref, pb_ref,
               q_out, k_out, v_out, a_out, n1_out, r1_out, dg_out, n2_out, r2_out, xb_out,
               small_out, big_out, a1_out, ax_out, qm_out, qw_out, wide_out, rp_out, pay_out, *rest):
    row_outs, rest = rest[:cut.GX], rest[cut.GX:]
    acts = rest[:cut.C]
    (x, wqkv, wo, w1, w2, wqkv1, wo1, w11, w21, wp,
     q, k, v, a, c, n1, r1, hb, dg, n2, r2, xb, h1, acc, first, act, factors, sem, osem) = rest[cut.C:]
    core = place()[1]
    PH = lab_ref.shape[0]
    tokens = lambda s: len_ref[s // PH, s % PH]
    T, D = x.shape
    S = T // 64
    FF = w1.shape[1]
    loads = [(x_hbm, x)]
    for part in range(3):
        cols = pl.ds(part * D, D)
        loads.append((wqkv_hbm.at[0, :, cols], wqkv.at[part]))
    loads += [(wo_hbm.at[0], wo), (w1_hbm.at[0], w1), (w2_hbm.at[0], w2)]
    for part in range(3):
        cols = pl.ds(part * D, D)
        loads.append((wqkv_hbm.at[1, :, cols], wqkv1.at[part]))
    loads += [(wo_hbm.at[1], wo1), (w1_hbm.at[1], w11), (w2_hbm.at[1], w21), (wp_hbm, wp)]
    copies = [pltpu.make_async_copy(s, d, sem.at[i]) for i, (s, d) in enumerate(loads)]
    for copy in copies[:4]:
        copy.start()
    stores = []

    def store(src, dst):
        copy = pltpu.make_async_copy(src, dst, osem.at[len(stores)])
        copy.start()
        stores.append(copy)

    copies[0].wait()
    TILE = D
    for part, dst in enumerate((q, k, v)):
        copies[1 + part].wait()
        for copy in (copies[4:6], copies[6:7], copies[7:])[part]:
            copy.start()

        def project(j, _, part=part, dst=dst):
            cols = pl.ds(pl.multiple_of(j * TILE, TILE), TILE)
            p = dot(x[...], wqkv[part, :, cols])
            if part == 0:
                p = (p + bias_ref[0:1, 0, cols]) * SCALE
            if part == 2:
                p = p + bias_ref[1:2, 0, cols]
            dst[:, cols] = p.astype(BF)
            return 0

        lax.fori_loop(0, D // TILE, project, 0)
    store(q, q_out)
    store(k, k_out)
    store(v, v_out)

    key = lax.broadcasted_iota(jnp.int32, (128, 256), 0)
    query = lax.broadcasted_iota(jnp.int32, (128, 256), 1)
    lane = lax.broadcasted_iota(jnp.int32, (128, 128), 1)
    low = lane < HD

    def attend(p, _):
        rows = pl.ds(pl.multiple_of(p * 128, 128), 128)
        i = 2 * p
        limit = jnp.where(key < 64, len_ref[i // PH, i % PH], len_ref[i // PH, i % PH + 1] + 64)
        keep = ((key // 64) == ((query // 64) % 2)) & (key < limit)
        for j in range(D // 128):
            lanes = slice(128 * j, 128 * j + 128)
            qq = q[rows, lanes]
            qm = jnp.concatenate([jnp.where(low, qq, 0), jnp.where(low, 0, qq)], 0)
            s = jnp.where(keep, dot(k[rows, lanes], qm, NT), MASKED)
            e = jnp.exp(s - jnp.max(s, 0, keepdims=True))
            prob = (e * (1.0 / jnp.sum(e, 0, keepdims=True))).astype(BF)
            a[p * (D // 128) + j] = prob
            ctx = dot(prob, v[rows, lanes], TN)
            c[rows, lanes] = jnp.where(low, ctx[:128], ctx[128:]).astype(BF)
        return 0

    lax.fori_loop(0, S // 2, attend, 0)
    store(a, a_out)
    by_core(cut, c, act, 5)
    by_core(cut, x, act, 6)

    copies[4].wait()
    ROWS = 256

    def first_norm(i, _):
        rows = pl.ds(pl.multiple_of(i * ROWS, ROWS), ROWS)
        z = x[rows, :].astype(F32) + dot(c[rows, :], wo[...]) + bias_ref[2:3, 0, :]
        n, r = normalize(z)
        n1[rows, :] = n.astype(BF)
        r1[rows, :] = jnp.broadcast_to(r, (ROWS, 128))
        h = n * gain_ref[0, 0:1, :] + bias_ref[3:4, 0, :]
        h1[rows, :] = h
        hb[rows, :] = h.astype(BF)
        acc[rows, :] = h + bias_ref[4:5, 0, :]
        return 0

    lax.fori_loop(0, T // ROWS, first_norm, 0)
    store(n1, n1_out)
    store(r1, r1_out)
    by_core(cut, hb, act, 4)
    copies[5].wait()
    copies[6].wait()

    WIDE = D // cut.C

    def widen(j, _):
        cols = pl.ds(pl.multiple_of(j * D, D), D)
        f = dot(hb[...], w1[:, cols]) + wb_ref[0:1, cols]
        gj, dgj = gelu_pair(f)
        gj = gj.astype(BF)
        dg[:, cols] = dgj.astype(BF)
        for half in range(cut.C):
            act[j % cut.C, j // cut.C * cut.C + half] = gj[:, half * WIDE:(half + 1) * WIDE]
        acc[...] += dot(gj, w2[cols, :])
        return 0

    lax.fori_loop(0, FF // D, widen, 0)
    store(dg, dg_out)
    store(act.at[core], acts[0])
    if cut.C == 2:
        store(act.at[1 - core], acts[1])

    def second_norm(i, _):
        rows = pl.ds(pl.multiple_of(i * ROWS, ROWS), ROWS)
        n, r = normalize(acc[rows, :])
        n2[rows, :] = n.astype(BF)
        r2[rows, :] = jnp.broadcast_to(r, (ROWS, 128))
        h = n * gain_ref[0, 1:2, :] + bias_ref[5:6, 0, :]
        acc[rows, :] = h
        xb[rows, :] = h.astype(BF)
        return 0

    lax.fori_loop(0, T // ROWS, second_norm, 0)
    store(n2, n2_out)
    store(r2, r2_out)
    store(xb, xb_out)

    for s in range(S):
        first[s:s + 1, :] = acc[64 * s:64 * s + 1, :]
    x0 = first[...]
    x0b = x0.astype(BF)
    for i in (7, 8, 9):
        copies[i].wait()
    q0 = ((dot(x0b, wqkv1[0]) + bias_ref[0:1, 1, :]) * SCALE).astype(BF)
    qm = head_rows(q0.astype(F32)).astype(BF)
    qw = dot(qm, wqkv1[1], NT).astype(BF)
    xall = xb[...]
    scores = dot(qw, xall, NT)
    row = lax.broadcasted_iota(jnp.int32, scores.shape, 0) % S
    col = lax.broadcasted_iota(jnp.int32, scores.shape, 1)
    keep = jnp.zeros(scores.shape, jnp.bool_)
    for s in range(S):
        keep = keep | ((row == s) & (col >= 64 * s) & (col < 64 * s + tokens(s)))
    scores = jnp.where(keep, scores, MASKED)
    e = jnp.exp(scores - jnp.max(scores, 1, keepdims=True))
    prob = e * (1.0 / jnp.sum(e, 1, keepdims=True))
    probb = prob.astype(BF)
    ax = dot(probb, xall).astype(BF)
    c0 = (head_fold(dot(ax, wqkv1[2])) + bias_ref[1:2, 1, :]).astype(BF)
    copies[10].wait()
    n10, r10 = normalize(x0 + dot(c0, wo1[...]) + bias_ref[2:3, 1, :])
    h10 = n10 * gain_ref[1, 0:1, :] + bias_ref[3:4, 1, :]
    h10b = h10.astype(BF)
    copies[11].wait()
    f0 = dot(h10b, w11[...]) + wb_ref[1:2, :]
    g0, dg0 = gelu_pair(f0)
    g0b = g0.astype(BF)
    copies[12].wait()
    n20, r20 = normalize(h10 + dot(g0b, w21[...]) + bias_ref[4:5, 1, :])
    x20 = n20 * gain_ref[1, 1:2, :] + bias_ref[5:6, 1, :]
    e0 = x20.astype(BF)
    copies[13].wait()
    rp = dot(e0, wp[...]) + pb_ref[...].reshape(1, D)
    rp_out[...] = rp
    squashed = jnp.tanh(rp)
    unit = squashed * lax.rsqrt(jnp.sum(squashed * squashed, -1, keepdims=True) + EPS_UNIT)
    row = lax.broadcasted_iota(jnp.int32, (S, 128), 0)
    lane = lax.broadcasted_iota(jnp.int32, (S, 128), 1)
    tail = jnp.zeros((S, 128), F32)
    for s in range(S):
        if s < PH:
            label = lab_ref[s]
            tail = jnp.where((row == s) & (lane == 0), (label // 32).astype(F32), tail)
            tail = jnp.where((row == s) & (lane == 1), (label % 32).astype(F32), tail)
        tail = jnp.where((row == s) & (lane == 2), tokens(s).astype(F32), tail)
    pay_out[...] = jnp.concatenate([unit, tail], 1).astype(BF)
    small_out[0] = n10
    small_out[1] = n20
    small_out[2] = jnp.broadcast_to(r10, n10.shape)
    small_out[3] = jnp.broadcast_to(r20, n10.shape)
    wide_out[...] = dg0
    big_out[:, 0:D] = c0
    big_out[:, D:2 * D] = x0b
    for i in range(cut.GX):
        lanes = slice(i * D // cut.GX, (i + 1) * D // cut.GX)
        factors[i] = jnp.concatenate([e0[:, lanes], h10b[:, lanes], g0b[:, i * FF // cut.GX:(i + 1) * FF // cut.GX]], 1)
    for r, out in enumerate(row_outs):
        out[...] = factors[place()[0] ^ r] if cut.GX > 1 else factors[0]
    a1_out[...] = probb
    ax_out[...] = ax
    qm_out[...] = qm
    qw_out[...] = qw
    for copy in stores:
        copy.wait()


def forward(cut, x, lengths, labels, wqkv, wo, w1, w2, wp, bias, gains, wb, pb):
    T, D = x.shape
    S = T // 64
    FF = w1.shape[2]
    nb = (S // 2) * (D // 128)
    sd = jax.ShapeDtypeStruct
    hbm = pl.BlockSpec(memory_space=pltpu.HBM)
    vm = pl.BlockSpec(memory_space=pltpu.VMEM)
    td = sd((T, D), BF)
    tr = sd((T, 128), F32)
    outs = [td, td, td, sd((nb, 128, 256), BF), td, tr, sd((T, FF), BF), td, tr, td,
            sd((4, S, D), F32), sd((S, 2 * D), BF), sd((H * S, T), BF), sd((H * S, D), BF),
            sd((H * S, D), BF), sd((H * S, D), BF), sd((S, FF), F32), sd((S, D), F32), sd((S, D + 128), BF)]
    outs += [sd((S, 6 * D // cut.GX), BF)] * cut.GX
    outs += [sd((7, T, D // cut.C), BF)] * cut.C
    out_specs = [hbm] * 10 + [vm] * (9 + cut.GX) + [hbm] * cut.C
    V = pltpu.VMEM
    b, r = V((T, D), BF), V((T, 128), F32)
    scratch = [b, V((3, D, D), BF), V((D, D), BF), V((D, FF), BF), V((FF, D), BF),
               V((3, D, D), BF), V((D, D), BF), V((D, FF), BF), V((FF, D), BF), V((D, D), BF),
               b, b, b, V((nb, 128, 256), BF), b, b, r, b, V((T, FF), BF), b, r, b,
               V((T, D), F32), V((T, D), F32), V((S, D), F32), V((cut.C, 7, T, D // cut.C), BF),
               V((cut.GX, S, 6 * D // cut.GX), BF),
               pltpu.SemaphoreType.DMA((14,)), pltpu.SemaphoreType.DMA((12,))]
    return pl.pallas_call(
        functools.partial(fwd_kernel, cut), out_shape=outs, out_specs=out_specs,
        in_specs=[pl.BlockSpec(memory_space=pltpu.SMEM)] * 2 + [hbm] * 6 + [vm] * 4,
        scratch_shapes=scratch, name="encode",
        compiler_params=pltpu.CompilerParams(vmem_limit_bytes=55 << 20),
    )(lengths, labels, x, wqkv, wo, w1, w2, wp, bias, gains, wb, pb)


HBM = pl.BlockSpec(memory_space=pltpu.HBM)
VM = pl.BlockSpec(memory_space=pltpu.VMEM)
SM = pl.BlockSpec(memory_space=pltpu.SMEM)


def norm_back(grad, n, root, gain):
    gn = grad * gain
    inner = jnp.mean(gn * n, -1, keepdims=True)
    return root * (gn - jnp.mean(gn, -1, keepdims=True) - n * inner)


def total_rows(values):
    return jnp.sum(values, 0, keepdims=True)


def runs(mode):
    return [(axis, mode.index(axis), mode.count(axis)) for axis in sorted(set(mode), reverse=True)]


def emit(cut, mode, parts, outs):
    if cut.C == 1:
        outs[0][...] = parts[0][...]
        return
    side = dict(zip("yx", place()[2:4]))
    for i, (axis, _, _) in enumerate(runs(mode)):
        bit = side[axis]
        outs[2 * i][...] = parts[i][bit]
        outs[2 * i + 1][...] = parts[i][1 - bit]


def pieces(cut, mode, rows, lanes):
    if cut.C == 1:
        return [pltpu.VMEM((1, 1, 1, rows, lanes), BF)], [sds((1, 1, 1, rows, lanes), BF)]
    scratch = [pltpu.VMEM((2, 2, n, rows, lanes), BF) for _, _, n in runs(mode)]
    return scratch, [sds((2, n, rows, lanes), BF) for _, _, n in runs(mode) for _ in range(2)]


def put(cut, mode, parts, y, x, z, value, rows=slice(None), lanes=slice(None)):
    if cut.C == 1:
        parts[0][0, 0, 0, rows, lanes] = value
        return
    for part, (axis, start, n) in zip(parts, runs(mode)):
        if start <= z < start + n:
            first, second = (y, x) if axis == "y" else (x, y)
            part[first, second, z - start, rows, lanes] = value


def start_all(pairs, sem):
    copies = [pltpu.make_async_copy(s, d, sem.at[i]) for i, (s, d) in enumerate(pairs)]
    for copy in copies:
        copy.start()
    return copies


def join(refs, out):
    out[...] = jnp.concatenate([ref[...].astype(F32) for ref in refs], 0).astype(BF)


def top_kernel(cut, PH, count, extra, gain_ref, *refs):
    local, (wqkv_hbm, wo_hbm, w1_hbm, w2_hbm, wp_hbm), rest = refs[:15], refs[15:20], refs[20:]
    bufs, rest = rest[-16:-1], rest[:-16] + rest[-1:]
    (own_ref, rp_ref, small_ref, big_ref, dg_ref, a1_ref, ax_ref, qm_ref, qw_ref, xb_ref, n2_ref, r2_ref,
     n1_ref, r1_ref, dg0_ref) = bufs
    early = start_all(list(zip(local, bufs)), rest[-1].at[pl.ds(7, 15)])
    gathered = rest[:count]
    join(rest[count:count + cut.GX], rest[count + extra])
    rest = rest[:count + extra] + rest[count + extra + 1:]
    (loss_out, tot_out, gy_out, vec_out, eb_out, gf_out, eb0_out, gz1_out, gc_out, vec2_out), rest = (
        rest[count + extra:count + extra + 10], rest[count + extra + 10:])
    (stay_out, go_out), rest = (rest[0], rest[1 if cut.C == 2 else 0]), rest[cut.C:]
    wqkv, wo, w1, w2, wp, gx, left_s, sem = rest
    D = wo.shape[0]
    FF = w1.shape[1]
    for copy in early[:12]:
        copy.wait()
    S = own_ref.shape[0]
    R = sum(g.shape[0] for g in gathered)
    T = xb_ref.shape[0]
    loads = [(wp_hbm, wp), (w2_hbm.at[1], w2), (w1_hbm.at[1], w1), (wo_hbm.at[1], wo)]
    for p in range(3):
        loads.append((wqkv_hbm.at[1, :, pl.ds(p * D, D)], wqkv.at[p]))
    copies = [pltpu.make_async_copy(s, d, sem.at[i]) for i, (s, d) in enumerate(loads)]
    for copy in copies:
        copy.start()
    gxi, gyi = place()[0], place()[5]
    me = gxi * lax.axis_size("gy") + gyi

    def device(j):
        r = j // S
        if cut.C == 1:
            return r
        flips = ((r // 8) % 2 * 2 + r // 16) * 8 + r % 4 * 2 + (r // 4) % 2
        return me ^ flips


    everyone = jnp.concatenate([g[...] for g in gathered], 0) if count > 1 else gathered[0][...]
    units = everyone[:, 0:D]
    extra = everyone[:, D:D + 128]
    i8 = lax.broadcasted_iota(jnp.int32, (8, 128), 0)
    l8 = lax.broadcasted_iota(jnp.int32, (8, 128), 1)
    pick = jnp.where((i8 == 0) & (l8 == 0), 32.0, 0.0) + jnp.where((i8 == 0) & (l8 == 1), 1.0, 0.0)
    pick = pick + jnp.where((i8 == 1) & (l8 == 2), 1.0, 0.0)
    meta = dot(pick.astype(BF), extra, NT)
    label_row = meta[0:1, :]
    tokens = jnp.sum(meta[1:2, :], 1, keepdims=True)
    tot_out[...] = jnp.broadcast_to(tokens, tot_out.shape)
    parts = []
    BLK = min(R, 256)
    for b in range(R // BLK):
        mat = SCORE * dot(units, units[b * BLK:(b + 1) * BLK, :], NT)
        j = lax.broadcasted_iota(jnp.int32, (R, BLK), 0)
        target = (j % S) >= PH
        pair = (device(j) * PH + (j % S) - PH).astype(F32)
        chosen = target & (pair == label_row[:, b * BLK:(b + 1) * BLK])
        logits = jnp.where(target, mat - jnp.where(chosen, SCORE * MARGIN, 0.0), -1e30)
        top = jnp.max(logits, 0, keepdims=True)
        parts.append(top + jnp.log(jnp.sum(jnp.exp(logits - top), 0, keepdims=True)))
    lse_row = jnp.concatenate(parts, 1) if len(parts) > 1 else parts[0]
    own_units = own_ref[:, 0:D]
    own_extra = own_ref[:, D:D + 128].astype(F32)
    own_label = 32.0 * own_extra[:, 0:1] + own_extra[:, 1:2]
    mat = SCORE * dot(own_units, units, NT)
    j = lax.broadcasted_iota(jnp.int32, (S, R), 1)
    r = lax.broadcasted_iota(jnp.int32, (S, R), 0)
    target = (j % S) >= PH
    pair = (device(j) * PH + (j % S) - PH).astype(F32)
    chosen = target & (pair == own_label)
    logits = jnp.where(target, mat - jnp.where(chosen, SCORE * MARGIN, 0.0), -1e30)
    top = jnp.max(logits, 1, keepdims=True)
    lse = top + jnp.log(jnp.sum(jnp.exp(logits - top), 1, keepdims=True))
    loss = lse - jnp.sum(jnp.where(chosen, logits, 0.0), 1, keepdims=True)
    loss_out[...] = jnp.broadcast_to(loss, loss_out.shape)
    from_source = jnp.where(target, jnp.exp(logits - lse), 0.0) - jnp.where(chosen, 1.0, 0.0)
    pair_own = (me * PH + r - PH).astype(F32)
    source = (j % S) < PH
    chosen_t = source & (label_row == pair_own)
    logits_t = mat - jnp.where(chosen_t, SCORE * MARGIN, 0.0)
    from_target = jnp.where(source, jnp.exp(jnp.where(source, logits_t - lse_row, 0.0)), 0.0)
    from_target = from_target - jnp.where(chosen_t, 1.0, 0.0)
    glog = jnp.where(r < PH, from_source, from_target).astype(BF)
    gu = SCORE * dot(glog, units)
    squashed = jnp.tanh(rp_ref[...])
    rs = lax.rsqrt(jnp.sum(squashed * squashed, -1, keepdims=True) + EPS_UNIT)
    gt = rs * (gu - squashed * (rs * rs * jnp.sum(gu * squashed, -1, keepdims=True)))
    gr = (gt * (1.0 - squashed * squashed)).astype(BF)
    copies[0].wait()
    gx2 = dot(gr, wp[...], NT)

    n1, n2, r1, r2 = small_ref[0], small_ref[1], small_ref[2], small_ref[3]
    gz2 = norm_back(gx2, n2, r2, gain_ref[1, 1:2, :])
    gy = gz2.astype(BF)
    copies[1].wait()
    gf = (dot(gy, w2[...], NT) * dg_ref[...]).astype(BF)
    again = [pltpu.make_async_copy(w2_hbm.at[0], w2, sem.at[22])]
    again[0].start()
    copies[2].wait()
    gh1 = gz2 + dot(gf, w1[...], NT)
    again.append(pltpu.make_async_copy(w1_hbm.at[0], w1, sem.at[23]))
    again[1].start()
    gz1 = norm_back(gh1, n1, r1, gain_ref[1, 0:1, :])
    go = gz1.astype(BF)
    copies[3].wait()
    gc = dot(go, wo[...], NT).astype(BF).astype(F32)
    again.append(pltpu.make_async_copy(wo_hbm.at[0], wo, sem.at[24]))
    again[2].start()
    gcm = head_rows(gc).astype(BF)
    for i in (4, 5, 6):
        copies[i].wait()
    gcw = dot(gcm, wqkv[2], NT).astype(BF)
    xall = xb_ref[...]
    prob = a1_ref[...].astype(F32)
    ga = dot(gcw, xall, NT)
    gs = (prob * (ga - jnp.sum(ga * prob, 1, keepdims=True))).astype(BF)
    mm = dot(gs, xall).astype(BF)
    gpq = head_fold(dot(mm, wqkv[1])).astype(BF).astype(F32) * SCALE
    gpqb = gpq.astype(BF)
    back = dot(jnp.concatenate([gs, a1_ref[...]], 0), jnp.concatenate([qw_ref[...], gcw], 0), TN)
    gx[...] = back
    first = gz1 + dot(gpqb, wqkv[0], NT)
    for s in range(S):
        gx[64 * s:64 * s + 1, :] += first[s:s + 1, :]

    nx = n2_ref[...].astype(F32)
    gxv = gx[...]
    gzx = norm_back(gxv, nx, r2_ref[:, 0:1], gain_ref[0, 1:2, :])
    gyx = gzx.astype(BF)
    gy_out[...] = gyx
    for copy in early[12:]:
        copy.wait()
    again[0].wait()
    again[1].wait()
    gx[...] = gzx

    def feed(i, _):
        cols = pl.ds(pl.multiple_of(i * D, D), D)
        part = (dot(gy_out[...], w2[cols, :], NT) * dg0_ref[:, cols].astype(F32)).astype(BF)
        gf_out[:, cols] = part
        eb0_out[0:1, cols] = total_rows(part.astype(F32))
        gx[...] += dot(part, w1[:, cols], NT)
        return 0

    lax.fori_loop(0, FF // D, feed, 0)
    gh = gx[...]
    n10 = n1_ref[...].astype(F32)
    gz10 = norm_back(gh, n10, r1_ref[:, 0:1], gain_ref[0, 0:1, :])
    gz1_out[...] = gz10
    go0 = gz10.astype(BF)
    gf_out[:, FF:] = go0
    vec2_out[0:1, :] = total_rows(gh)
    vec2_out[1:2, :] = total_rows(gh * n10)
    vec2_out[2:3, :] = total_rows(go0.astype(F32))
    vec2_out[3:8, :] = jnp.zeros((5, D), F32)
    again[2].wait()
    gc_out[...] = dot(go0, wo[...], NT).astype(BF)

    vec_out[0:1, :] = total_rows(gpqb.astype(F32))
    vec_out[1:2, :] = total_rows(gc)
    vec_out[2:3, :] = total_rows(go.astype(F32))
    vec_out[3:4, :] = total_rows(gh1)
    vec_out[4:5, :] = total_rows(gy.astype(F32))
    vec_out[5:6, :] = total_rows(gx2)
    vec_out[6:7, :] = total_rows(gh1 * n1)
    vec_out[7:8, :] = total_rows(gx2 * n2)
    vec_out[8:9, :] = total_rows(gr.astype(F32))
    vec_out[9:10, :] = total_rows(gxv)
    vec_out[10:11, :] = total_rows(gxv * nx)
    vec_out[11:12, :] = total_rows(gyx.astype(F32))
    vec_out[12:16, :] = jnp.zeros((4, D), F32)
    eb_out[...] = total_rows(gf.astype(F32))

    width = D // cut.GX
    cut_up = lambda v: [v[:, i * width:(i + 1) * width] for i in range(v.shape[1] // width)]
    c0, x0 = big_ref[:, 0:D].astype(F32), big_ref[:, D:2 * D].astype(F32)
    mmf, axf = mm.astype(F32), ax_ref[...].astype(F32)
    for g in range(cut.GX):
        lanes = slice(g * width, (g + 1) * width)
        blocks = [v[h * S:(h + 1) * S, lanes] for v in (mmf, axf) for h in range(H)]
        blocks += [x0[:, lanes], c0[:, lanes]]
        dst = g if cut.C == 1 else g ^ gxi
        for i, block in enumerate(blocks):
            left_s[dst, i] = block.astype(BF)
    q0 = head_fold(qm_ref[...].astype(F32))
    right = cut_up(gpq) + cut_up(q0) + cut_up(gc) + cut_up(go.astype(F32))
    grf, gyf, gff = gr.astype(F32), gy.astype(F32), gf.astype(F32)
    dn, df = D // cut.GY, FF // cut.GY
    for g in range(cut.GY):
        mix = jnp.concatenate([grf[:, g * dn:(g + 1) * dn], gyf[:, g * dn:(g + 1) * dn],
                               gff[:, g * df:(g + 1) * df]], 1)
        right += cut_up(mix)
    right = [block.astype(BF) for block in right]
    L = LEFT
    for out, base in (((stay_out, 0), (go_out, 2)) if cut.C == 2 else ((stay_out, 0),)):
        for r in range(cut.C):
            out[r * L:(r + 1) * L] = left_s[base + r]
        for i, block in enumerate(right):
            out[cut.C * L + i] = block


LEFT = 2 * H + 2


def params(mb):
    return pltpu.CompilerParams(vmem_limit_bytes=mb << 20)


def cost(weight=0.0):
    return pl.CostEstimate(flops=int(weight * UNIT), bytes_accessed=1, transcendentals=0)


UNIT = 10 ** 10
MODE = {2: "yyxx", 3: "yyyy", 4: "yyxx"}
LONG = 1000.0


def call(kernel, name, mb, outs, ins, hbm=(), smem=(), scratch=(), after=(), weight=0.0):
    hbm = [in_hbm(t) for t in hbm]
    return pl.pallas_call(
        functools.partial(kernel), out_shape=list(outs), name=name,
        in_specs=[SM] * len(smem) + [VM] * len(ins) + [HBM] * (len(hbm) + len(after)), out_specs=[VM] * len(outs),
        scratch_shapes=list(scratch), compiler_params=params(mb), cost_estimate=cost(weight),
    )(*smem, *ins, *hbm, *after)


def in_hbm(t):
    return pltpu.with_memory_space_constraint(t, pltpu.HBM)


def sds(shape, dtype):
    return jax.ShapeDtypeStruct(shape, dtype)


def top(cut, after, factors, gathered, own, rp, small, big, dg, a1, ax, qm, qw, xb, n2, r2, n1, r1, dg0, gains, wqkv, wo, w1, w2, wp):
    S = own.shape[0]
    T, D = xb.shape
    FF = w1.shape[2]
    width = D // cut.GX
    V = pltpu.VMEM
    count = cut.C * LEFT + 4 * cut.GX + (2 * D + FF) // width
    td = sds((T, D), BF)
    after = [*factors, *after]
    outs = [sds((S * cut.GX, factors[0].shape[1]), BF), sds((S, 128), F32), sds((8, 128), F32), td, sds((16, D), F32), sds((1, FF), F32), sds((T, FF + D), BF),
            sds((1, FF), F32), sds((T, D), F32), td, sds((8, D), F32)] + [sds((count, S, width), BF)] * cut.C
    local = (own, rp, small, big, dg, a1, ax, qm, qw, xb, n2, r2, n1, r1, dg0)
    bufs = [V(t.shape, t.dtype) for t in local]
    return pl.pallas_call(
        functools.partial(top_kernel, cut, S // 2, len(gathered), len(after)), out_shape=outs,
        in_specs=[VM] + [HBM] * 20 + [VM] * (len(gathered) + cut.GX) + [HBM] * (len(after) - cut.GX), out_specs=[VM] * len(outs),
        scratch_shapes=[V((3, D, D), BF), V((D, D), BF), V((D, FF), BF), V((FF, D), BF), V((D, D), BF),
                        V((T, D), F32), V((cut.GX, LEFT, S, width), BF), *bufs, pltpu.SemaphoreType.DMA((25,))],
        name="rank_and_top_back", compiler_params=params(44 if cut.C == 2 else 58), cost_estimate=cost(),
    )(gains, *(in_hbm(t) for t in (*local, wqkv, wo, w1, w2, wp)), *gathered, *after)


def peers_of(cut, refs):
    L = LEFT
    if cut.C == 1:
        return [(refs[0], 0, L)]
    stay, got_y, got_c = refs
    n = stay.shape[0] - 2 * L
    return [(stay, 0, 2 * L), (got_y, 0, 2 * L), (got_c, 0, 2 * L), (got_c, L, 2 * L + n)]


def top_weights_kernel(cut, S, count, *refs):
    peers = peers_of(cut, refs[:count])
    outs = refs[count:]
    sides = cut.X
    chunks, part, stage = outs[:sides], outs[-2], outs[-1]
    xbit = place()[3] if sides == 2 else 0
    width = refs[0].shape[2]
    D = width * cut.GX
    G = cut.GX
    get = lambda ref, i: ref[i].astype(F32)
    lane_cat = lambda ref, i, m: jnp.concatenate([get(ref, i + k) for k in range(m)], 1) if m > 1 else get(ref, i)
    rights = [[lane_cat(ref, ro + k * G, G) for k in range(4)] for ref, lo, ro in peers]
    low = lax.broadcasted_iota(jnp.int32, (S, 128), 1) < HD
    stack = lambda pieces: jnp.concatenate(pieces, 0).astype(BF)
    cols = [dot(stack([get(ref, lo + 2 * H) for ref, lo, ro in peers]), stack([r[0] for r in rights]), TN)]
    for kind in range(2):
        for j in range(D // 128):
            lhs, rhs = [], []
            for (ref, lo, ro), r in zip(peers, rights):
                lhs += [get(ref, lo + kind * H + 2 * j), get(ref, lo + kind * H + 2 * j + 1)]
                blk = r[kind + 1][:, 128 * j:128 * j + 128]
                rhs += [jnp.where(low, blk, 0.0), jnp.where(low, 0.0, blk)]
            cols.append(dot(stack(lhs), stack(rhs), TN))
    qkv = jnp.concatenate(cols, 1)
    out = dot(stack([get(ref, lo + 2 * H + 1) for ref, lo, ro in peers]), stack([r[3] for r in rights]), TN)
    wa, wb = 3 * D // cut.GY, D // cut.GY
    halves = []
    for x in range(sides):
        blocks = []
        for z in range(cut.Z):
            b = z * sides + x
            blocks.append(jnp.concatenate(
                [qkv[:, b * wa:(b + 1) * wa], out[:, b * wb:(b + 1) * wb]], 1).astype(BF))
        halves.append(blocks)
    for z in range(cut.Z):
        for x in range(sides):
            part[x, z] = halves[x][z]
    for r, dst in enumerate(chunks):
        for z in range(cut.Z):
            dst[z * width:(z + 1) * width, :] = part[xbit ^ r, z] if sides == 2 else part[0, z]
    m = (2 * D + 4 * D) // cut.GY // width
    if sides == 1:
        ref, lo, ro = peers[0]
        outs[1][...] = ref[ro + 4 * G:ro + 4 * G + m]
        return
    n = cut.Z * width
    for r, dst in enumerate(chunks):
        x = xbit ^ r
        for p, (ref, lo, ro) in enumerate(peers):
            lanes = slice(p % 2 * width, (p % 2 + 1) * width)
            for z in range(cut.Z):
                for i in range(m):
                    to = n + ((z * 2 + p // 2) * m + i) * S
                    piece = ref[pl.ds(ro + 4 * G + (z * sides + x) * m + i, 1)]
                    stage[to - n:to - n + S, lanes] = piece[0].astype(F32)
        dst[n:, :] = stage[...].astype(BF)


def top_weights(cut, arrays, left=(), after=()):
    S, width = arrays[0].shape[1:]
    D = width * cut.GX
    peers = 4 if cut.C == 2 else 1
    m = 6 * D // cut.GY // width
    lanes = 4 * D // cut.GY
    extra = cut.Z * (peers // 2) * m * S
    outs = [sds((cut.Z * width + extra, lanes), BF)] * cut.X
    if cut.C == 1:
        outs.append(sds((m, S, width), BF))
    n = len(arrays)
    if cut.C == 2:
        outs.append(sds((2 * left[0].shape[0], left[0].shape[1]), BF))

    def kernel(*refs):
        ins, (left_a, left_b), refs = refs[:n], refs[n:n + 2] if left else (None, None), refs[n + len(left) + len(after):]
        if left:
            refs[cut.X][0:left_a.shape[0], :] = left_a[...]
            refs[cut.X][left_a.shape[0]:, :] = left_b[...]
            refs = refs[:cut.X] + refs[cut.X + 1:]
        top_weights_kernel(cut, S, n, *ins, *refs)

    return call(kernel, "top_weights", 20, outs, [*arrays, *left], after=after,
                scratch=[pltpu.VMEM((cut.X, cut.Z, width, lanes), BF), pltpu.VMEM((max(extra, 8), lanes), F32)], weight=LONG)


def pack_kernel(stay, got, left_a, left_b, *rest):
    out, left_out = rest[-2:]
    left_out[0:left_a.shape[0], :] = left_a[...]
    left_out[left_a.shape[0]:, :] = left_b[...]
    L = LEFT
    n = stay.shape[0] - 2 * L
    for src, lo, dst, m in ((stay, L, 0, L), (got, L, L, L), (stay, 2 * L, 2 * L, n), (got, 2 * L, 2 * L + n, n)):
        out[dst:dst + m] = src[lo:lo + m]


def pack(stay, got, left, left_got, after=()):
    n = 2 * (stay.shape[0] - LEFT)
    outs = [sds((n,) + stay.shape[1:], BF), sds((2 * left.shape[0], left.shape[1]), BF)]
    return call(pack_kernel, "pack", 8, outs, (stay, got, left, left_got), after=after)


def row_weights_kernel(cut, lefts, rights, pool_out, expand_out, reduce_out):
    dk = lefts[0].shape[-1] // 6
    D = dk * cut.GX
    dn = D // cut.GY
    if cut.C == 2:
        rows = []
        for d in range(4):
            ref, base = rights[d // 2], (0, dk)[d // 2]
            for s in range(2):
                for p in range(4):
                    at = base + d % 2 * 96 + s * 48 + p // 2 * 24
                    lanes = slice(p % 2 * dk, (p % 2 + 1) * dk)
                    rows.append(jnp.concatenate([ref[at + 8 * i:at + 8 * i + 8, lanes].astype(F32) for i in range(3)], 1))
        own, got = lefts
        n, lanes = own.shape[0], got.shape[1]
        blocks = [got[got.shape[0] - (3 - i) * n:got.shape[0] - (2 - i) * n, :] for i in range(3)]
        right = jnp.concatenate(rows, 0).astype(BF)
        near = jnp.concatenate([b.astype(F32) for b in blocks], 1).astype(BF)
        h = n // 2
        left = jnp.concatenate([own[0:h, :], near[0:h, :], own[h:, :], near[h:, :]], 0)
    else:
        left = lefts[0][...]
        right = jnp.concatenate([rights[0][i] for i in range(rights[0].shape[0])], 1)
    pool_out[...] = dot(left[:, 0:dk], right[:, 0:dn], TN)
    expand_out[...] = dot(left[:, dk:2 * dk], right[:, 2 * dn:], TN)
    reduce_out[...] = dot(right[:, dn:2 * dn], left[:, 2 * dk:], TN)


def row_weights(cut, lefts, rights, after=()):
    dk = lefts[0].shape[-1] // 6
    dn = dk * cut.GX // cut.GY
    outs = [sds((dk, dn), F32), sds((dk, 4 * dn), F32), sds((dn, 4 * dk), F32)]
    m, n = len(lefts), len(lefts) + len(rights)
    kernel = lambda *refs: row_weights_kernel(cut, refs[:m], refs[m:n], *refs[n + len(after):])
    return call(kernel, "row_weights", 32, outs, (*lefts, *rights), after=after)


def narrow_weight_kernel(cut, *refs):
    C = cut.C
    mode = MODE[2]
    m = 2 * C + (2 * len(runs(mode)) if C == 2 else 1)
    gys, acts, outs, parts, turned = refs[:C], refs[C:2 * C], refs[2 * C:m], refs[m:-1], refs[-1]
    T, D = acts[0].shape[1], acts[0].shape[2] * C
    nw = D // cut.GY
    width = D // C
    for c in range(C):
        turned[c] = gys[c][...].T

    def weigh(b, _):
        res = dot(turned[0], acts[0][b])
        for c in range(1, C):
            res = res + dot(turned[c], acts[c][b])
        res = res.astype(BF)
        for x in range(cut.X):
            for z in range(cut.Z):
                g = z * cut.X + x
                value = res[g * nw:(g + 1) * nw, :]
                if C == 1:
                    put(cut, mode, parts, 0, x, z, value, lanes=pl.ds(pl.multiple_of(b * width, 128), width))
                else:
                    put(cut, mode, parts, b // 2, x, z, value, pl.ds(pl.multiple_of(b % 2 * nw, 16), nw))
        return 0

    lax.fori_loop(0, 4, weigh, 0)
    emit(cut, mode, parts, outs)


def narrow_weight(cut, gys, acts, after=()):
    D = acts[0].shape[2] * cut.C
    scratch, outs = pieces(cut, MODE[2], cut.C * D // cut.GY, 4 * D // cut.GX // cut.C)
    n = 2 * cut.C
    kernel = lambda *refs: narrow_weight_kernel(cut, *refs[:n], *refs[n + len(after):])
    return call(kernel, "narrowing_weight", 24, outs, (*gys, *acts), after=after,
                scratch=scratch + [pltpu.VMEM((cut.C, D, gys[0].shape[0]), BF)])


def widen_weight_kernel(cut, *refs):
    C = cut.C
    mode = MODE[3]
    m = 2 * C + (2 * len(runs(mode)) if C == 2 else 1)
    acts, gfs, outs, parts = refs[:C], refs[C:2 * C], refs[2 * C:m], refs[m:]
    width = acts[0].shape[2]
    D = width * C
    FF = gfs[0].shape[1] - D
    lw, kr = FF // cut.GY, D // cut.GX
    left = [a[4].T for a in acts]
    W = D
    for i in range(FF // W):
        res = dot(left[0], gfs[0][:, i * W:(i + 1) * W])
        for c in range(1, C):
            res = res + dot(left[c], gfs[c][:, i * W:(i + 1) * W])
        res = res.astype(BF)
        if C == 1:
            put(cut, mode, parts, 0, 0, 0, res, lanes=slice(i * W, (i + 1) * W))
            continue
        for h in range(W // lw):
            g = i * W // lw + h
            for y in range(cut.Y):
                put(cut, mode, parts, y, g % cut.X, g // cut.X, res[y * kr:(y + 1) * kr, h * lw:(h + 1) * lw])
    emit(cut, mode, parts, outs)


def widen_weight_back(cut, acts, gfs, after=()):
    D = acts[0].shape[2] * cut.C
    FF = gfs[0].shape[1] - D
    scratch, outs = pieces(cut, MODE[3], D // cut.GX, FF // cut.GY)
    n = 2 * cut.C
    kernel = lambda *refs: widen_weight_kernel(cut, *refs[:n], *refs[n + len(after):])
    return call(kernel, "widening_weight", 24, outs, (*acts, *gfs), after=after, scratch=scratch)


def attend_kernel(extra, gc, q, k, v, a, vec1, vec2, eb0, eb1, *rest):
    gp = rest[-1]
    T, D = q.shape
    S = T // 64
    lane = lax.broadcasted_iota(jnp.int32, (128, 128), 1)
    low = lane < HD
    NB = D // 128

    def heads(p, _):
        rows = pl.ds(pl.multiple_of(p * 128, 128), 128)
        for j in range(NB):
            lanes = slice(128 * j, 128 * j + 128)
            gcj = gc[rows, lanes]
            gcm = jnp.concatenate([jnp.where(low, gcj, 0), jnp.where(low, 0, gcj)], 0)
            qj = q[rows, lanes]
            qm = jnp.concatenate([jnp.where(low, qj, 0), jnp.where(low, 0, qj)], 0)
            pb = a[p * NB + j]
            prob = pb.astype(F32)
            gp[rows, 2 * D + 128 * j:2 * D + 128 * j + 128] = dot(pb, gcm).astype(BF)
            ga = dot(v[rows, lanes], gcm, NT)
            gs = (prob * (ga - jnp.sum(ga * prob, 0, keepdims=True))).astype(BF)
            gp[rows, D + 128 * j:D + 128 * j + 128] = dot(gs, qm).astype(BF)
            gq = dot(gs, k[rows, lanes], TN)
            gq = jnp.where(low, gq[:128], gq[128:]).astype(BF)
            gp[rows, lanes] = (gq.astype(F32) * SCALE).astype(BF)
        return 0

    lax.fori_loop(0, S // 2, heads, 0)
    one = lambda ref, i: ref[i:i + 1, :]
    vecs = [total_rows(gp[0:T, 0:D].astype(F32)), total_rows(gp[0:T, 2 * D:3 * D].astype(F32)),
            one(vec2, 2), one(vec2, 0), one(vec1, 11), one(vec1, 9)]
    vecs += [one(vec1, i) for i in range(6)] + [one(vec2, 1), one(vec1, 10), one(vec1, 6), one(vec1, 7), one(vec1, 8)]
    vecs += [jnp.zeros((1, D), F32)] * (32 - len(vecs))
    gp[T:T + 16, :] = jnp.zeros((16, 3 * D), BF)
    block = jnp.concatenate([jnp.concatenate(vecs[8 * i:8 * i + 8], 0) for i in range(3)], 1)
    wide = jnp.concatenate([eb[:, i * D:(i + 1) * D] for eb in (eb0, eb1) for i in range(4)], 0)
    wide = jnp.concatenate([wide, jnp.zeros((8, 2 * D), F32)], 1)
    gp[T:T + 16, :] = jnp.concatenate([block, wide], 0).astype(BF)


def attend_back(gc, q, k, v, a, vectors, after=()):
    T, D = gc.shape
    return call(functools.partial(attend_kernel, len(after)), "attention_back", 30,
                [sds((T + 16, 3 * D), BF)], (gc, q, k, v, a, *vectors), after=after, weight=LONG)


def acts_width(ref, C):
    return ref.shape[2] * C


class Lanes:
    def __init__(self, refs):
        self.refs, self.rows, self.width = refs, refs[0].shape[0], refs[0].shape[1]

    def get(self, rows, start, stop):
        w = self.width
        found = [self.refs[i][rows, max(start - i * w, 0):min(stop - i * w, w)]
                 for i in range(start // w, (stop + w - 1) // w)]
        return jnp.concatenate(found, 1) if len(found) > 1 else found[0]


def attend_weight_kernel(cut, *refs):
    C = cut.C
    mode = MODE[4]
    n = 1
    acts, gos, gps = refs[:C], refs[C:2 * C], [Lanes(refs[2 * C + c * n:2 * C + (c + 1) * n]) for c in range(C)]
    refs = refs[2 * C + C * n:]
    m = 2 * len(runs(mode)) if C == 2 else 1
    outs, parts, blocks = refs[:m], refs[m:-1], refs[-1]
    width = acts[0].shape[2]
    D = width * C
    T = gps[0].rows - 16
    ct = [a[5].T for a in acts]
    xt = [a[6].T for a in acts]
    wa, wb = 3 * D // cut.GY, D // cut.GY
    main = wa // 128 * 128
    tail = wa - main
    kr = D // cut.GX

    def place_rows(res, x, z, lanes):
        res = res.astype(BF)
        for y in range(cut.Y):
            put(cut, mode, parts, y, x, z, res[y * kr:(y + 1) * kr, :], slice(0, kr), lanes)

    both = lambda f: f(0) + f(1) if C == 2 else f(0)
    if cut.GY == 1:
        place_rows(dot(xt[0], gps[0].get(slice(0, T), 0, 3 * D)), 0, 0, slice(0, 3 * D))
        place_rows(dot(ct[0], gos[0][:, 4 * D:]), 0, 0, slice(3 * D, None))
        emit(cut, mode, parts, outs)
        return
    for x in range(cut.X):
        for z in range(cut.Z):
            a0 = (z * cut.X + x) * wa
            place_rows(both(lambda c: dot(xt[c], gps[c].get(slice(0, T), a0, a0 + main))), x, z, slice(0, main))
    order = [(x, z) for x in range(cut.X) for z in range(cut.Z)]
    for i in range(0, len(order), 2):
        def tails(c):
            ra, rb = [], []
            for x, z in order[i:i + 2]:
                g = z * cut.X + x
                a0, o0 = g * wa, 4 * D + g * wb
                ra += [gps[c].get(slice(0, T), a0 + main, a0 + wa), jnp.zeros((T, 128 - tail), BF)]
                rb += [jnp.zeros((T, tail), BF), gos[c][:, o0:o0 + wb]]
            return dot(xt[c], jnp.concatenate(ra, 1)) + dot(ct[c], jnp.concatenate(rb, 1))
        res = both(tails)
        for m, (x, z) in enumerate(order[i:i + 2]):
            place_rows(res[:, 128 * m:128 * m + 128], x, z, slice(main, wa + wb))
    core = place()[1]
    vec = both(lambda c: gps[c].get(slice(T, T + 16), 0, 3 * D).astype(F32))
    n = 4 * 8
    dv, dw = D // n, 4 * D // n
    for d in range(n):
        pieces = [vec[0:8, k * D + d * dv:k * D + (d + 1) * dv] for k in range(3)]
        row, at = d * dw // D, d * dw % D
        pieces += [jnp.zeros((8, 128 - 3 * dv), F32), vec[8 + row:9 + row, at:at + dw], vec[12 + row:13 + row, at:at + dw]]
        pieces[-2:] = [jnp.concatenate(pieces[-2:] + [jnp.zeros((6, dw), F32)], 0),
                       jnp.zeros((8, wa + wb - 128 - dw), F32)]
        blocks[d] = jnp.concatenate([jnp.concatenate(pieces, 1), jnp.zeros((8, wa + wb), F32)], 0).astype(BF)
    for y in range(cut.Y):
        for x in range(cut.X):
            for z in range(cut.Z):
                put(cut, mode, parts, y, x, z, blocks[(2 * y + core) * 8 + z * cut.X + x], slice(kr, kr + 16))
    emit(cut, mode, parts, outs)


def attend_weight(cut, acts, gyos, gps, after=()):
    D = acts[0].shape[2] * cut.C
    D4 = 4 * D
    kr = D // cut.GX + (16 if cut.C == 2 else 0)
    scratch, outs = pieces(cut, MODE[4], kr, D4 // cut.GY)
    ins = [*acts, *gyos, *(part for parts in gps for part in parts)]
    n = len(ins)
    kernel = lambda *refs: attend_weight_kernel(cut, *refs[:n], *refs[n + len(after):])
    return call(kernel, "attention_weight", 30, outs, ins, after=after,
                scratch=scratch + [pltpu.VMEM((32, 16, D4 // cut.GY), BF)])


def input_kernel(pairs, extra, len_ref, tot_ref, gz_ref, *rest):
    n = 1
    gp, w_hbm, (gx_out, sc_out, w, sem) = Lanes(rest[:n]), rest[n], rest[n + 1 + extra:]
    T, D = gz_ref.shape
    PH = len_ref.shape[1]
    copies = start_all([(w_hbm.at[0, :, pl.ds(i * D, D)], w.at[i]) for i in range(3)], sem)
    for copy in copies:
        copy.wait()
    gx_out[...] = gz_ref[...]

    def project(i, _):
        gx_out[...] += dot(gp.refs[0][0:T, pl.ds(pl.multiple_of(i * D, D), D)], w[i], NT)
        return 0

    lax.fori_loop(0, 3, project, 0)
    inverse = 1.0 / tot_ref[0:1, 0:1]
    for s in range(T // 64):
        rows = slice(64 * s, 64 * s + 64)
        factor = (2.0 * pairs) * len_ref[s // PH, s % PH].astype(F32) * inverse
        sc_out[rows, :] = gx_out[rows, :] * factor


def input_back(pairs, lengths, tot, gz1, gp, wqkv, after=()):
    T, D = gz1.shape
    return call(functools.partial(input_kernel, pairs, len(after)), "input_back", 24, [sds((T, D), F32)] * 2,
                (tot, gz1, *gp), (wqkv,), (lengths,),
                scratch=[pltpu.VMEM((3, D, D), BF), pltpu.SemaphoreType.DMA((3,))], after=after, weight=LONG)


def plus(a, b):
    return (a.astype(F32) + b.astype(F32)).astype(BF)


def flip(values, axis, bits):
    return lax.ppermute(values, axis, [(i, i ^ bits) for i in range(lax.axis_size(axis))])


def fold_kernel(mode, extra, *refs):
    n = 2 * len(runs(mode))
    ins, outs = refs[:n], refs[n + extra:]
    side = dict(zip("yx", place()[2:4]))
    for i, (axis, _, _) in enumerate(runs(mode)):
        bit = side["x" if axis == "y" else "y"]
        keep, got = ins[2 * i:2 * i + 2]
        mine, other = outs[2 * i:2 * i + 2]
        other[...] = plus(keep[1 - bit], got[1 - bit])
        mine[...] = plus(keep[bit], got[bit])


def spread_kernel(mode, extra, *refs):
    n = 2 * len(runs(mode))
    ins, left, (keep_out, send_out, total) = refs[:n], refs[n], refs[n + 1 + extra:]
    low = lax.rem(place()[4], 2)
    for i, (_, start, count) in enumerate(runs(mode)):
        total[start:start + count] = plus(ins[2 * i][...], ins[2 * i + 1][...])
    rows, lanes = total.shape[1:]
    for dst, parity in ((send_out, 1 - low), (keep_out, low)):
        for high in range(2):
            dst[high * rows:(high + 1) * rows] = total[high * 2 + parity]
    m = left.shape[0]
    for i in range(left.shape[1] // lanes):
        send_out[2 * rows + i * m:2 * rows + (i + 1) * m] = left[:, i * lanes:(i + 1) * lanes]


def spread(mode, ins, left, after=()):
    rows, lanes = ins[0].shape[-2:]
    keep, send = call(functools.partial(spread_kernel, mode, len(after)), "spread", 16,
                      [sds((2 * rows, lanes), BF), sds((2 * rows + left.size // lanes, lanes), BF)], [*ins, left],
                      after=after, scratch=[pltpu.VMEM((4, rows, lanes), BF)])
    return keep, flip(send, "gy", 2), send


def spread_rows_kernel(extra, kr, keep, got, *rest):
    keep_out, send_out = rest[extra:]
    low = lax.rem(place()[4], 2)
    m = (keep.shape[0] - 4 * kr) // 4
    for dst, parity in ((send_out, 1 - low), (keep_out, low)):
        for high in range(2):
            z = high * 2 + parity
            at = high * (kr + 2 * m)
            rows = pl.ds(pl.multiple_of(z * kr, 16), kr)
            dst[at:at + kr] = plus(keep[rows, :], got[rows, :])
            rows = pl.ds(pl.multiple_of(4 * kr + z * m, 16), m)
            dst[at + kr:at + kr + m] = keep[rows, :]
            dst[at + kr + m:at + kr + 2 * m] = got[rows, :]


def spread_rows(keep, got, kr, after=()):
    shape = sds((2 * kr + keep.shape[0] - 4 * kr, keep.shape[1]), BF)
    keep, send = call(functools.partial(spread_rows_kernel, len(after), kr), "spread_rows", 16, [shape] * 2,
                      (keep, got), after=after)
    return keep, flip(send, "gy", 2), send


def settle_two_kernel(extra, kr, keep, got, keep2, got2, *rest):
    own_out, rows_out, own2_out, send_out = rest[extra:]
    high = lax.div(place()[4], 2)
    n = keep.shape[0] // 2
    m = n - kr
    part = lambda ref, h, start, size: ref[pl.ds(pl.multiple_of(h * n + start, 16), size), :]
    send_out[0:kr] = plus(part(keep, 1 - high, 0, kr), part(got, 1 - high, 0, kr))
    own_out[...] = part(keep, high, 0, kr).astype(F32) + part(got, high, 0, kr).astype(F32)
    for i, src in enumerate((keep, got)):
        send_out[kr + i * m:kr + (i + 1) * m] = part(src, 1 - high, kr, m)
        rows_out[i * m:(i + 1) * m] = part(src, high, kr, m)
    r2 = keep2.shape[0] // 2
    two = lambda ref, h: ref[pl.ds(pl.multiple_of(h * r2, 16), r2), :]
    send_out[kr + 2 * m:] = plus(two(keep2, 1 - high), two(got2, 1 - high))
    own2_out[...] = two(keep2, high).astype(F32) + two(got2, high).astype(F32)


def settle_two(keep, got, keep2, got2, kr, after=()):
    lanes, m = keep.shape[1], keep.shape[0] - 2 * kr
    r2 = keep2.shape[0] // 2
    outs = [sds((kr, lanes), F32), sds((m, lanes), BF), sds((r2, lanes), F32), sds((kr + m + r2, lanes), BF)]
    own, rows, own2, send = call(functools.partial(settle_two_kernel, len(after), kr), "settle_two", 16, outs,
                                 (keep, got, keep2, got2), after=after, weight=0.1)
    return own, rows, own2, flip(send, "gy", 4)


def spread_two_kernel(modes, extra, *refs):
    count = [2 * len(runs(mode)) for mode in modes]
    ins, outs = refs[:sum(count)], refs[sum(count) + extra:]
    low = lax.rem(place()[4], 2)
    for k, mode in enumerate(modes):
        keep_out, send_out, total = outs[2 * k], outs[2 * k + 1], outs[4 + k]
        for i, (_, start, n) in enumerate(runs(mode)):
            total[start:start + n] = plus(ins[2 * i][...], ins[2 * i + 1][...])
        ins = ins[2 * len(runs(mode)):]
        for dst, parity in ((send_out, 1 - low), (keep_out, low)):
            for high in range(2):
                dst[high] = total[high * 2 + parity]


def spread_two(first, second, after=()):
    ins = [first.operands(), second.operands()]
    tails = [t[0].shape[-2:] for t in ins]
    outs = call(functools.partial(spread_two_kernel, (first.mode, second.mode), len(after)), "spread_two", 16,
                [sds((2,) + t, BF) for t in tails for _ in range(2)], ins[0] + ins[1], after=after,
                scratch=[pltpu.VMEM((4,) + t, BF) for t in tails])
    return [outs[0], flip(outs[1], "gy", 2), outs[2], flip(outs[3], "gy", 2)], outs[1]


def settle_last_kernel(extra, keep3, got3, keep4, got4, *rest):
    own_out, send_out = rest[extra:]
    high = lax.div(place()[4], 2)
    n = keep3.shape[1]
    for keep, got, rows in ((keep3, got3, slice(0, n)), (keep4, got4, slice(n, None))):
        send_out[rows, :] = plus(keep[1 - high], got[1 - high])
        own_out[rows, :] = keep[high].astype(F32) + got[high].astype(F32)


def settle_last(ins, after=()):
    shape = (ins[0].shape[1] + ins[2].shape[1], ins[0].shape[2])
    own, send = call(functools.partial(settle_last_kernel, len(after)), "settle_last", 16,
                     [sds(shape, F32), sds(shape, BF)], ins, after=after)
    return own, flip(send, "gy", 4), send


def cross(values, axis):
    return flip(values, "gy", 1) if axis == "x" else flip(values, "gx", 2)


class Share:
    def __init__(self, chunk, mode):
        self.mode = mode
        self.keep = chunk[0::2]
        self.got = [cross(t, axis) for t, (axis, _, _) in zip(chunk[1::2], runs(mode))]

    def operands(self):
        return [t for pair in zip(self.keep, self.got) for t in pair]

    def fold(self, *after):
        outs = call(functools.partial(fold_kernel, self.mode, len(after)), "fold", 16,
                    [sds(t.shape[1:], BF) for t in self.keep for _ in range(2)], self.operands(), after=after)
        self.keep = outs[0::2]
        self.got = [cross(t, "x" if axis == "y" else "y") for t, (axis, _, _) in zip(outs[1::2], runs(self.mode))]
        return outs[1]

    def spread(self, left, *after):
        return spread(self.mode, self.operands(), left, after)


def finish_wide_kernel(own2, got12, own34, got34, r1, e1, reduce_out, expand_out):
    n = own2.shape[0]
    two = own2[...] + got12[got12.shape[0] - n:, :].astype(F32)
    reduce_out[0] = jnp.concatenate([two[0:n // 2], two[n // 2:]], 1)
    reduce_out[1] = r1[...]
    expand_out[0] = own34[0:n, :] + got34[0:n, :].astype(F32)
    expand_out[1] = e1[...]


def finish_attend_kernel(wa, own34, got34, own1, got12, *outs):
    attend_out, output_out, bias_out, gains_out, wb_out, pb_out = outs
    kr = own1.shape[0]
    a, b = own34[kr:, :] + got34[kr:, :].astype(F32), own1[...] + got12[0:kr, :].astype(F32)
    for layer, v in enumerate((a[0:kr], b)):
        attend_out[layer] = v[:, 0:wa]
        output_out[layer] = v[:, wa:]
    vec = a[kr:kr + 8, :]
    dv = bias_out.shape[2]
    one = lambda i: vec[i % 8:i % 8 + 1, i // 8 * dv:i // 8 * dv + dv]
    for layer in range(2):
        for i in range(6):
            bias_out[i, layer:layer + 1, :] = one(6 * layer + i)
        for i in range(2):
            gains_out[layer, i:i + 1, :] = one(12 + 2 * layer + i)
    wb_out[...] = vec[0:2, 128:128 + 4 * dv]
    pb_out[...] = one(16)


def scatter(values, row_axis, col_axis):
    part = lax.psum_scatter(values.astype(BF), row_axis, scatter_dimension=0, tiled=True)
    return lax.psum_scatter(part, col_axis, scatter_dimension=1, tiled=True).astype(F32)


def shards(mesh, inputs, lengths, labels, wqkv, wo, w1, w2, bias, gains, wb, wp, pb):
    GX, GY = mesh.shape["gx"], mesh.shape["gy"]
    n = GX * GY
    near = (GX, GY) == (4, 8)
    cut = Cut(2, 2, 2, 4) if near else Cut(1, 1, 1, 1)
    PH = labels.shape[0]
    S = 2 * PH
    L, D = inputs.shape[2], inputs.shape[3]
    T = S * L
    FF = w1.shape[2]
    twin = lambda v: [v, flip(v, "gx", 1)] if near else [v]
    x = inputs.reshape(T, D)
    (q, k, v, a, n1, r1, dg, n2, r2, xb, small, big, a1, ax, qm, qw, dg1, rp, own, *rest) = forward(
        cut, x, lengths, labels, wqkv, wo, w1, w2, wp, bias.transpose(1, 0, 2), gains, wb, pb)
    factors, acts = rest[:cut.GX], rest[cut.GX:]
    if near:
        factors = [flip(factors[r], "gx", r) if r else factors[0] for r in (0, 2, 1, 3)]
        line = jnp.concatenate([own] + [flip(own, "gy", 2 * d) for d in (1, 2, 3)], 0)
        corner = lax.ppermute(line, ("gx", "gy"), [(i, i ^ 17) for i in range(n)])
        plane = jnp.concatenate([line, flip(line, "gy", 1), flip(line, "gx", 2), corner], 0)
        gathered = [plane, flip(plane, "gx", 1)]
        acts = [acts[0], flip(acts[1], "gx", 1)]
    else:
        gathered = [lax.all_gather(own, ("gx", "gy"), axis=0, tiled=True)]
    left, loss, tot, gy, vec1, eb1, gfo, eb0, gz1, gc, vec2, *rows = top(
        cut, acts[1:], factors, gathered, own, rp, small, big, dg1, a1, ax, qm, qw, xb, n2, r2, n1, r1, dg, gains, wqkv, wo, w1, w2, wp)
    gfs, vectors = twin(gfo), (vec1, vec2, eb0, eb1)
    shape = (2, PH, L, D)
    wa = 3 * D // GY
    gys = twin(gy)
    if near:
        stay, go_y = rows
        got_y = cross(go_y, "y")
        ch2 = narrow_weight(cut, gys, acts)
        s2 = Share(ch2, MODE[2])
        gp = attend_back(gc, q, k, v, a, vectors, (ch2[0],))
        gps = twin(gp[0])
        packed, left = pack(stay, got_y, left, cross(left, "x"), (gp[0],))
        ch3 = widen_weight_back(cut, acts, gfs, (packed,))
        s3 = Share(ch3, MODE[3])
        t = s2.fold(ch3[0])
        ch1 = top_weights(cut, [stay, got_y, flip(packed, "gx", 1)], (left, flip(left, "gy", 4)), (t,))
        got1 = cross(ch1[1], "x")
        ch4 = attend_weight(cut, acts, gfs, [[t] for t in gps], (ch1[0],))
        keep2, got2, t = s2.spread(ch1[2], ch4[0])
        left = [ch1[2], got2]
        t = s3.fold(t, got1)
        s4 = Share(ch4, MODE[4])
        kr, dn, dv = D // GX, D // GY, D // n
        keep1, got1, t = spread_rows(ch1[0], got1, kr, (t,))
        gx0, sc0 = input_back(n * PH, lengths, tot, gz1, gp, wqkv, (t,))
        t = s4.fold(gx0)
        own1, rows1, own2, got12 = settle_two(keep1, got1, keep2, got2, kr, (t,))
        last, t = spread_two(s3, s4, (rows1,))
        own34, got34, t = settle_last(last, (t, got12))
        d_pool, d_expand1, d_reduce1 = row_weights(cut, left, [rows1, got12], (t,))
        d_reduce, d_expand = call(
            finish_wide_kernel, "finish_wide", 16, [sds((2, dn, FF // GX), F32), sds((2, kr, FF // GY), F32)],
            (own2, got12, own34, got34, d_reduce1, d_expand1))
        d_reduce = d_reduce.transpose(0, 2, 1)
        d_attend, d_output, d_bias, d_gains, d_wb, d_pb = call(
            functools.partial(finish_attend_kernel, wa), "finish_attend", 16,
            [sds((2, kr, wa), F32), sds((2, kr, dn), F32), sds((6, 2, dv), F32), sds((2, 2, dv), F32),
             sds((2, FF // n), F32), sds((1, dv), F32)], (own34, got34, own1, got12))
        d_bias, d_pb = d_bias.transpose(1, 0, 2), d_pb.reshape(dv)
    else:
        ch2 = narrow_weight(cut, gys, acts)
        ch3 = widen_weight_back(cut, acts, gfs)
        ch1 = top_weights(cut, rows)
        gp = attend_back(gc, q, k, v, a, vectors)
        ch4 = attend_weight(cut, acts, gfs, [gp])
        gx0, sc0 = input_back(n * PH, lengths, tot, gz1, gp, wqkv)
        f1, f2, f3, f4 = (t[0].reshape(t[0].shape[-2:]) for t in (ch1, ch2, ch3, ch4))
        pool, expand1, reduce1 = row_weights(cut, [left], ch1[1:])
        d_attend = jnp.stack([scatter(t[:, :3 * D], "gx", "gy") for t in (f4, f1)])
        d_output = jnp.stack([scatter(t[:, 3 * D:], "gx", "gy") for t in (f4, f1)])
        d_expand = jnp.stack([scatter(t, "gx", "gy") for t in (f3, expand1)])
        d_reduce = jnp.stack([scatter(t, "gy", "gx").T for t in (f2, reduce1)])
        d_pool = scatter(pool, "gx", "gy")
        me = lax.axis_index("gx") * GY + lax.axis_index("gy")
        sums = lax.psum(jnp.concatenate([t[T:] for t in gp], 1).astype(F32), ("gx", "gy"))
        vec = sums[0:8].reshape(8, 3, D).transpose(1, 0, 2).reshape(24, D)
        vec = lax.dynamic_slice_in_dim(vec, me * (D // n), D // n, 1)
        d_bias, d_gains, d_pb = vec[0:12].reshape(2, 6, -1), vec[12:16].reshape(2, 2, -1), vec[16]
        d_wb = lax.dynamic_slice_in_dim(sums[8:16, :D].reshape(2, FF), me * (FF // n), FF // n, 1)
    return (loss[:PH, 0], gx0.reshape(shape), sc0.reshape(shape), d_attend, d_output, d_expand, d_reduce,
            d_bias, d_gains, d_wb, d_pool, d_pb)


def solution(mesh):
    both = ("gx", "gy")
    in_specs = (P(None, both, None, None), P(None, both), P(both)) + (P(),) * 9
    out_specs = (P(both), P(None, both, None, None), P(None, both, None, None), P(None, "gx", "gy"),
                 P(None, "gx", "gy"), P(None, "gx", "gy"), P(None, "gx", "gy"), P(None, None, both),
                 P(None, None, both), P(None, both), P("gx", "gy"), P(both))
    return jax.shard_map(functools.partial(shards, mesh), mesh=mesh, in_specs=in_specs, out_specs=out_specs,
                         check_vma=False)
```

profile of v0, /device:TPU:0, one launch (start us, length us, event | category | flops | bytes accessed | tf_op | source)
XLA Modules:
  0.0 205.0 jit_solution(13906763017698370418)
XLA Ops:
  0.7 24.3 %encode.1 = (bf16[512,768]{1,0:T(8,128)(2,1)}, bf16[512,768]{1,0:T(8,128)(2,1)}, bf16[512,768]{1,0:T(8,128)(2,1)}, bf16[24,128,256]{2,1,0:T(8,128)(2,1)}, bf16[5...) custom-call(s32[2,4]{1,0:T(2,128)} %len_ref.3, ...), custom_call_target="tpu_custom_call" | custom-call | tf_op jit(solution)/shard_map/encode/pallas_call | solution.py:310
  25.5 2.6 %collective-permute-start = (bf16[8,896]{1,0:T(8,128)(2,1)}, bf16[8,896]{1,0:T(8,128)(2,1)S(1)}, u32[]{:S(2)}, u32[]{:S(2)}) collective-permute-start(bf16[8,896]{1,0:T(8,128)(2,1)} %get-tuple-element.102.refs_0_), channel_id=1, source_target_pairs={{0,2},{1,3},{2,0},{3,1},{4,6},{5,7},{6,4},{7,5},{8,10},{9,11},{10,... | collective-permute-start | bytes 43016 | tf_op jit(solution)/shard_map/ppermute | solution.py:1022
  28.1 2.6 %collective-permute-start.1 = (bf16[8,896]{1,0:T(8,128)(2,1)}, bf16[8,896]{1,0:T(8,128)(2,1)S(1)}, u32[]{:S(2)}, u32[]{:S(2)}) collective-permute-start(bf16[8,896]{1,0:T(8,128)(2,1)} %get-tuple-element.102.refs_0_), channel_id=1, source_target_pairs={{0,4},{1,5},{2,6},{3,7},{4,0},{5,1},{6,2},{7,3},{8,12},{9,13},{10,... | collective-permute-start | bytes 43016 | tf_op jit(solution)/shard_map/ppermute | solution.py:1022
  31.5 1.4 collective-permute-done.1
  33.0 3.5 %collective-permute-done.2 = bf16[8,896]{1,0:T(8,128)(2,1)S(1)} collective-permute-done((bf16[8,896]{1,0:T(8,128)(2,1)}, bf16[8,896]{1,0:T(8,128)(2,1)S(1)}, u32[]{:S(2)}, u32[]{:S(2)}) %collective-permute-start.2) | collective-permute-done | bytes 14368 | tf_op jit(solution)/shard_map/ppermute | solution.py:1022
  36.4 1.5 collective-permute-start.3
  37.9 1.5 collective-permute-start.4
  39.9 1.1 collective-permute-done.3
  41.1 1.5 collective-permute-done.4
  42.6 2.0 collective-permute-done.5
  45.4 1.5 collective-permute-start.9
  46.8 1.9 collective-permute-done.7.refs_23_
  49.6 20.9 %rank_and_top_back.1 = (bf16[32,1152]{1,0:T(8,128)(2,1)}, f32[8,128]{1,0:T(8,128)S(1)}, f32[8,128]{1,0:T(8,128)S(1)}, bf16[512,768]{1,0:T(8,128)(2,1)S(1)}, f32[...) custom-call(f32[2,2,768]{2,1,0:T(2,128)S(1)} %copy-done.5, ...), custom_call_target="tpu_custom_call" | custom-call | bytes 1 | tf_op jit(solution)/shard_map/rank_and_top_back/pallas_call | solution.py:622
  70.8 1.5 collective-permute-start.12
  72.9 5.6 %narrowing_weight.1 = (bf16[2,2,192,384]{3,2,1,0:T(8,128)(2,1)S(1)}, bf16[2,2,192,384]{3,2,1,0:T(8,128)(2,1)}, bf16[2,2,192,384]{3,2,1,0:T(8,128)(2,1)S(1)}, bf16[2,2,192,384]{3,2,1,0:T(8,128)(2,1)}) custom-call(bf16[512,768]{1,0:T(8,128)(2,1)S(1)} %get-tuple-element.134.refs_0_, bf16[512,768]{1,0:T(8,128)(2,1)S(1)} %collective-permute-done.11.refs_1_, ...), custom_call_target="tpu_custom_call" | custom-call | bytes 1 | tf_op jit(solution)/shard_map/narrowing_weight/pallas_call | solution.py:594
  78.5 1.4 collective-permute-start.16
  80.5 8.5 %attention_back.1.rest_0_.refs_4_ = bf16[528,2304]{1,0:T(8,128)(2,1)} custom-call(bf16[512,768]{1,0:T(8,128)(2,1)S(1)} %get-tuple-element.125.gc, bf16[512,768]{1,0:T(8,128)(2,1)S(1)} %copy-done.9, bf16[512,768]{1,0:T(8,128)(2,1)S(1)} %copy-done.10, bf16[512,768]{1,0:T(8,128)(2,1)S(1)} %copy-done.11, bf16[24,128,256]{2,1,0:T(8,128)(2,1)S(1)} %copy-done.8, ...), custom_call_target="tpu_custom_call" | custom-call | flops 9999999827968 | bytes 1 | tf_op jit(solution)/shard_map/attention_back/pallas_call | solution.py:594
  89.0 1.1 pack.1
  90.7 2.1 %copy-done.2 = bf16[512,3840]{1,0:T(8,128)(2,1)S(1)} copy-done((bf16[512,3840]{1,0:T(8,128)(2,1)S(1)}, bf16[512,3840]{1,0:T(8,128)(2,1)}, u32[]{:S(2)}) %copy-start.2) | copy-done | bytes 3932184
  92.8 6.0 %widening_weight.1 = (bf16[2,4,192,384]{3,2,1,0:T(8,128)(2,1)S(1)}, bf16[2,4,192,384]{3,2,1,0:T(8,128)(2,1)}) custom-call(bf16[7,512,384]{2,1,0:T(8,128)(2,1)S(1)} %copy-done, bf16[7,512,384]{2,1,0:T(8,128)(2,1)S(1)} %collective-permute-done.10.refs_26_.refs_3_.refs_1_, bf16[512,3840]{1,0:T(8,128)(2,1)S(1)} %copy-done.2, ...), custom_call_target="tpu_custom_call" | custom-call | bytes 1 | tf_op jit(solution)/shard_map/widening_weight/pallas_call | solution.py:594
  98.8 1.5 collective-permute-start.20
  100.3 1.5 fold.3
  101.9 2.4 %top_weights.1 = (bf16[960,384]{1,0:T(8,128)(2,1)S(1)}, bf16[960,384]{1,0:T(8,128)(2,1)S(1)}, bf16[128,1152]{1,0:T(8,128)(2,1)S(1)}) custom-call(bf16[92,8,192]{2,1,0:T(8,128)(2,1)S(1)} %get-tuple-element.137.stay.refs_0_, bf16[92,8,192]{2,1,0:T(8,128)(2,1)} %collective-permute-done.12.got.refs_1_, bf16[132,8,192]{2,1,0:T(8,128)(2,1)S(1)} %collective-permute-done.14.refs_2_, ...), custom_call_target="tpu_custom_call" | custom-call | flops 9999999827968 | bytes 1 | tf_op jit(solution)/shard_map/top_weights/pallas_call | solution.py:594
  104.9 1.5 collective-permute-start.21
  106.9 2.1 %copy-done.3 = bf16[512,3840]{1,0:T(8,128)(2,1)S(1)} copy-done((bf16[512,3840]{1,0:T(8,128)(2,1)S(1)}, bf16[512,3840]{1,0:T(8,128)(2,1)}, u32[]{:S(2)}) %copy-start.3) | copy-done | bytes 3932184
  109.0 8.8 %attention_weight.1 = (bf16[2,2,208,384]{3,2,1,0:T(8,128)(2,1)S(1)}, bf16[2,2,208,384]{3,2,1,0:T(8,128)(2,1)}, bf16[2,2,208,384]{3,2,1,0:T(8,128)(2,1)S(1)}, bf16[2,2,208,384]{3,2,1,0:T(8,128)(2,1)}) custom-call(bf16[7,512,384]{2,1,0:T(8,128)(2,1)S(1)} %copy-done.1, bf16[7,512,384]{2,1,0:T(8,128)(2,1)S(1)} %collective-permute-done.10.refs_26_.refs_3_.refs_1_, ...), custom_call_target="tpu_custom_call" | custom-call | bytes 1 | tf_op jit(solution)/shard_map/attention_weight/pallas_call | solution.py:594
  117.8 1.5 collective-permute-start.25
  119.3 9.7 %collective-permute-done.21.refs_1_ = bf16[2,192,384]{2,1,0:T(8,128)(2,1)S(1)} collective-permute-done((bf16[2,192,384]{2,1,0:T(8,128)(2,1)S(1)}, bf16[2,192,384]{2,1,0:T(8,128)(2,1)S(1)}, u32[]{:S(2)}, u32[]{:S(2)}) %collective-permute-start.21) | collective-permute-done | bytes 294944 | tf_op jit(solution)/shard_map/ppermute | solution.py:1022
  129.5 4.7 %collective-permute-done.22.refs_3_ = bf16[2,192,384]{2,1,0:T(8,128)(2,1)S(1)} collective-permute-done((bf16[2,192,384]{2,1,0:T(8,128)(2,1)S(1)}, bf16[2,192,384]{2,1,0:T(8,128)(2,1)S(1)}, u32[]{:S(2)}, u32[]{:S(2)}) %collective-permute-start.22) | collective-permute-done | bytes 294944 | tf_op jit(solution)/shard_map/ppermute | solution.py:1022
  134.1 1.2 spread.1
  135.8 2.2 %fold.4 = (bf16[4,192,384]{2,1,0:T(8,128)(2,1)S(1)}, bf16[4,192,384]{2,1,0:T(8,128)(2,1)}) custom-call(bf16[2,4,192,384]{3,2,1,0:T(8,128)(2,1)S(1)} %get-tuple-element.146.refs_4_.refs_0_, bf16[2,4,192,384]{3,2,1,0:T(8,128)(2,1)} %collective-permute-done.20.refs_1_, bf16[768,384]{1,0:T(8,128)(2,1)} %get-tuple-element.156.refs_2_, ...), custom_call_target="tpu_custom_call" | custom-call | bytes 1 | tf_op jit(solution)/shard_map/fold/pallas_call | solution.py:594
  138.1 1.4 collective-permute-start.24
  140.3 1.5 collective-permute-start.29
  141.8 8.1 %input_back.1 = (f32[512,768]{1,0:T(8,128)}, f32[512,768]{1,0:T(8,128)}) custom-call(s32[2,4]{1,0:T(2,128)S(1)} %copy-done.7, f32[8,128]{1,0:T(8,128)S(1)} %get-tuple-element.123.tot_ref, f32[512,768]{1,0:T(8,128)S(1)} %get-tuple-element.124.gz_ref, bf16[528,2304]{1,0:T(8,128)(2,1)} %attention_back.1.rest_0_.refs_4_, bf16[2,768,2304]{2,1,0:T(8,128)(2,1)} %rest_1_.1, ...), custom_call_target="tpu_custom_call" | custom-call | flops 9999999827968 | bytes 1 | tf_op jit(solution)/shard_map/input_back/pallas_call | solution.py:594
  150.0 1.4 copy-done.4
  151.4 1.6 fold.5
  153.7 1.5 collective-permute-start.28
  155.2 3.7 %collective-permute-done.29.got = bf16[576,384]{1,0:T(8,128)(2,1)} collective-permute-done((bf16[576,384]{1,0:T(8,128)(2,1)}, bf16[576,384]{1,0:T(8,128)(2,1)}, u32[]{:S(2)}, u32[]{:S(2)}) %collective-permute-start.29) | collective-permute-done | bytes 442400 | tf_op jit(solution)/shard_map/ppermute | solution.py:1022
  158.9 1.3 settle_two.1
  160.2 3.2 %collective-permute-start.33 = (bf16[576,384]{1,0:T(8,128)(2,1)S(1)}, bf16[576,384]{1,0:T(8,128)(2,1)S(1)}, u32[]{:S(2)}, u32[]{:S(2)}) collective-permute-start(bf16[576,384]{1,0:T(8,128)(2,1)S(1)} %get-tuple-element.176), channel_id=1, source_target_pairs={{0,4},{1,5},{2,6},{3,7},{4,0},{5,1},{6,2},{7,3},{8,12},{9,13},{10,... | collective-permute-start | bytes 1327112 | tf_op jit(solution)/shard_map/ppermute | solution.py:1022
  164.0 1.7 spread_two.1
  165.8 0.9 collective-permute-start.32
  166.7 1.2 collective-permute-start.31
  167.9 21.3 %collective-permute-done.31.got3 = bf16[2,192,384]{2,1,0:T(8,128)(2,1)S(1)} collective-permute-done((bf16[2,192,384]{2,1,0:T(8,128)(2,1)S(1)}, bf16[2,192,384]{2,1,0:T(8,128)(2,1)S(1)}, u32[]{:S(2)}, u32[]{:S(2)}) %collective-permute-start.31) | collective-permute-done | bytes 294944 | tf_op jit(solution)/shard_map/ppermute | solution.py:1022
  190.0 2.2 %row_weights.1 = (f32[192,96]{1,0:T(8,128)}, f32[192,384]{1,0:T(8,128)S(1)}, f32[96,768]{1,0:T(8,128)S(1)}) custom-call(bf16[128,1152]{1,0:T(8,128)(2,1)S(1)} %get-tuple-element.154.refs_4_.refs_0_, bf16[768,384]{1,0:T(8,128)(2,1)} %collective-permute-done.30.got2.refs_1_, bf16[192,384]{1,0:T(8,128)(2,1)S(1)} %get-tuple-element.171.refs_6_.refs_2_, ...), custom_call_target="tpu_custom_call" | custom-call | bytes 1 | tf_op jit(solution)/shard_map/row_weights/pallas_call | solution.py:594
  192.2 10.7 %collective-permute-done.34.got34 = bf16[400,384]{1,0:T(8,128)(2,1)S(1)} collective-permute-done((bf16[400,384]{1,0:T(8,128)(2,1)S(1)}, bf16[400,384]{1,0:T(8,128)(2,1)S(1)}, u32[]{:S(2)}, u32[]{:S(2)}) %collective-permute-start.34) | collective-permute-done | bytes 307232 | tf_op jit(solution)/shard_map/ppermute | solution.py:1022
  202.9 1.0 finish_attend.1
  203.9 1.1 finish_wide.1
  (74 shorter events, 10.7 us)
Async XLA Ops:
  0.6 48.2 %copy-start.5 = (f32[2,2,768]{2,1,0:T(2,128)S(1)}, f32[2,2,768]{2,1,0:T(2,128)}, u32[]{:S(2)}) copy-start(f32[2,2,768]{2,1,0:T(2,128)} %gain_ref.3) | copy-start | bytes 36868
  25.0 23.9 %collective-permute-start.10 = (bf16[7,512,384]{2,1,0:T(8,128)(2,1)}, bf16[7,512,384]{2,1,0:T(8,128)(2,1)S(1)}, u32[]{:S(2)}, u32[]{:S(2)}) collective-permute-start(bf16[7,512,384]{2,1,0:T(8,128)(2,1)} %get-tuple-element.121), channel_id=1, source_target_pairs={{0,8},{8,0},{16,24},{24,16},{1,9},{9,1},{17,25},{25,17},{2,10},{10... | collective-permute-start | bytes 8257544 | tf_op jit(solution)/shard_map/ppermute | solution.py:1022
  25.5 6.0 %collective-permute-start = (bf16[8,896]{1,0:T(8,128)(2,1)}, bf16[8,896]{1,0:T(8,128)(2,1)S(1)}, u32[]{:S(2)}, u32[]{:S(2)}) collective-permute-start(bf16[8,896]{1,0:T(8,128)(2,1)} %get-tuple-element.102.refs_0_), channel_id=1, source_target_pairs={{0,2},{1,3},{2,0},{3,1},{4,6},{5,7},{6,4},{7,5},{8,10},{9,11},{10,... | collective-permute-start | bytes 43016 | tf_op jit(solution)/shard_map/ppermute | solution.py:1022
  28.1 4.8 %collective-permute-start.1 = (bf16[8,896]{1,0:T(8,128)(2,1)}, bf16[8,896]{1,0:T(8,128)(2,1)S(1)}, u32[]{:S(2)}, u32[]{:S(2)}) collective-permute-start(bf16[8,896]{1,0:T(8,128)(2,1)} %get-tuple-element.102.refs_0_), channel_id=1, source_target_pairs={{0,4},{1,5},{2,6},{3,7},{4,0},{5,1},{6,2},{7,3},{8,12},{9,13},{10,... | collective-permute-start | bytes 43016 | tf_op jit(solution)/shard_map/ppermute | solution.py:1022
  30.7 5.7 %collective-permute-start.2 = (bf16[8,896]{1,0:T(8,128)(2,1)}, bf16[8,896]{1,0:T(8,128)(2,1)S(1)}, u32[]{:S(2)}, u32[]{:S(2)}) collective-permute-start(bf16[8,896]{1,0:T(8,128)(2,1)} %get-tuple-element.102.refs_0_), channel_id=1, source_target_pairs={{0,6},{1,7},{2,4},{3,5},{4,2},{5,3},{6,0},{7,1},{8,14},{9,15},{10,... | collective-permute-start | bytes 43016 | tf_op jit(solution)/shard_map/ppermute | solution.py:1022
  36.4 4.6 %collective-permute-start.3 = (bf16[32,896]{1,0:T(8,128)(2,1)S(1)}, bf16[32,896]{1,0:T(8,128)(2,1)S(1)}, u32[]{:S(2)}, u32[]{:S(2)}) collective-permute-start(bf16[32,896]{1,0:T(8,128)(2,1)S(1)} %get-tuple-element.192), channel_id=1, source_target_pairs={{0,1},{1,0},{2,3},{3,2},{4,5},{5,4},{6,7},{7,6},{8,9},{9,8},{10,11... | collective-permute-start | bytes 172040 | tf_op jit(solution)/shard_map/ppermute | solution.py:1022
  37.9 4.6 %collective-permute-start.4 = (bf16[32,896]{1,0:T(8,128)(2,1)S(1)}, bf16[32,896]{1,0:T(8,128)(2,1)S(1)}, u32[]{:S(2)}, u32[]{:S(2)}) collective-permute-start(bf16[32,896]{1,0:T(8,128)(2,1)S(1)} %get-tuple-element.192), channel_id=1, source_target_pairs={{0,16},{8,24},{16,0},{24,8},{1,17},{9,25},{17,1},{25,9},{2,18},{10... | collective-permute-start | bytes 172040 | tf_op jit(solution)/shard_map/ppermute | solution.py:1022
  39.5 5.1 %collective-permute-start.5 = (bf16[32,896]{1,0:T(8,128)(2,1)S(1)}, bf16[32,896]{1,0:T(8,128)(2,1)S(1)}, u32[]{:S(2)}, u32[]{:S(2)}) collective-permute-start(bf16[32,896]{1,0:T(8,128)(2,1)S(1)} %get-tuple-element.192), channel_id=1, source_target_pairs={{0,17},{1,16},{2,19},{3,18},{4,21},{5,20},{6,23},{7,22},{8,25},{9,... | collective-permute-start | bytes 172040 | tf_op jit(solution)/shard_map/ppermute | solution.py:1222
  44.5 4.3 %collective-permute-start.6 = (bf16[128,896]{1,0:T(8,128)(2,1)S(1)}, bf16[128,896]{1,0:T(8,128)(2,1)S(1)}, u32[]{:S(2)}, u32[]{:S(2)}) collective-permute-start(bf16[128,896]{1,0:T(8,128)(2,1)S(1)} %constant_dynamic-update-slice_fusion.4.refs_20_), channel_id=1, source_target_pairs={{0,8},{8,0},{16,24},{24,16},{1,9},{9,1},{17,25},{25,17},{2,10},{10... | collective-permute-start | bytes 688136 | tf_op jit(solution)/shard_map/ppermute | solution.py:1022
  44.6 4.1 %collective-permute-start.7 = (bf16[8,1152]{1,0:T(8,128)(2,1)}, bf16[8,1152]{1,0:T(8,128)(2,1)S(1)}, u32[]{:S(2)}, u32[]{:S(2)}) collective-permute-start(bf16[8,1152]{1,0:T(8,128)(2,1)} %get-tuple-element.118), channel_id=1, source_target_pairs={{0,16},{8,24},{16,0},{24,8},{1,17},{9,25},{17,1},{25,9},{2,18},{10... | collective-permute-start | bytes 55304 | tf_op jit(solution)/shard_map/ppermute | solution.py:1022
  45.2 3.6 %collective-permute-start.8 = (bf16[8,1152]{1,0:T(8,128)(2,1)}, bf16[8,1152]{1,0:T(8,128)(2,1)S(1)}, u32[]{:S(2)}, u32[]{:S(2)}) collective-permute-start(bf16[8,1152]{1,0:T(8,128)(2,1)} %get-tuple-element.119), channel_id=1, source_target_pairs={{0,8},{8,0},{16,24},{24,16},{1,9},{9,1},{17,25},{25,17},{2,10},{10... | collective-permute-start | bytes 55304 | tf_op jit(solution)/shard_map/ppermute | solution.py:1022
  45.4 3.5 %collective-permute-start.9 = (bf16[8,1152]{1,0:T(8,128)(2,1)}, bf16[8,1152]{1,0:T(8,128)(2,1)S(1)}, u32[]{:S(2)}, u32[]{:S(2)}) collective-permute-start(bf16[8,1152]{1,0:T(8,128)(2,1)} %get-tuple-element.120), channel_id=1, source_target_pairs={{0,24},{8,16},{16,8},{24,0},{1,25},{9,17},{17,9},{25,1},{2,26},{10... | collective-permute-start | bytes 55304 | tf_op jit(solution)/shard_map/ppermute | solution.py:1022
  48.9 0.7 copy-start.6
  49.6 23.2 %copy-start = (bf16[7,512,384]{2,1,0:T(8,128)(2,1)S(1)}, bf16[7,512,384]{2,1,0:T(8,128)(2,1)}, u32[]{:S(2)}) copy-start(bf16[7,512,384]{2,1,0:T(8,128)(2,1)} %get-tuple-element.135.refs_2_.refs_0_) | copy-start | bytes 8257540
  70.5 2.4 %collective-permute-start.11 = (bf16[512,768]{1,0:T(8,128)(2,1)S(1)}, bf16[512,768]{1,0:T(8,128)(2,1)S(1)}, u32[]{:S(2)}, u32[]{:S(2)}) collective-permute-start(bf16[512,768]{1,0:T(8,128)(2,1)S(1)} %get-tuple-element.134.refs_0_), channel_id=1, source_target_pairs={{0,8},{8,0},{16,24},{24,16},{1,9},{9,1},{17,25},{25,17},{2,10},{10... | collective-permute-start | bytes 2359304 | tf_op jit(solution)/shard_map/ppermute | solution.py:1022
  70.8 18.2 %collective-permute-start.12 = (bf16[92,8,192]{2,1,0:T(8,128)(2,1)}, bf16[92,8,192]{2,1,0:T(8,128)(2,1)}, u32[]{:S(2)}, u32[]{:S(2)}) collective-permute-start(bf16[92,8,192]{2,1,0:T(8,128)(2,1)} %get-tuple-element.138), channel_id=1, source_target_pairs={{0,16},{8,24},{16,0},{24,8},{1,17},{9,25},{17,1},{25,9},{2,18},{10... | collective-permute-start | bytes 847880 | tf_op jit(solution)/shard_map/ppermute | solution.py:1022
  72.3 16.7 %collective-permute-start.13 = (bf16[32,1152]{1,0:T(8,128)(2,1)}, bf16[32,1152]{1,0:T(8,128)(2,1)}, u32[]{:S(2)}, u32[]{:S(2)}) collective-permute-start(bf16[32,1152]{1,0:T(8,128)(2,1)} %get-tuple-element.139.left_a), channel_id=1, source_target_pairs={{0,1},{1,0},{2,3},{3,2},{4,5},{5,4},{6,7},{7,6},{8,9},{9,8},{10,11... | collective-permute-start | bytes 221192 | tf_op jit(solution)/shard_map/ppermute | solution.py:1022
  72.8 17.4 %collective-permute-start.18 = (bf16[512,3840]{1,0:T(8,128)(2,1)}, bf16[512,3840]{1,0:T(8,128)(2,1)}, u32[]{:S(2)}, u32[]{:S(2)}) collective-permute-start(bf16[512,3840]{1,0:T(8,128)(2,1)} %get-tuple-element.145.refs_2_), channel_id=1, source_target_pairs={{0,8},{8,0},{16,24},{24,16},{1,9},{9,1},{17,25},{25,17},{2,10},{10... | collective-permute-start | bytes 11796488 | tf_op jit(solution)/shard_map/ppermute | solution.py:1022
  72.8 7.7 %copy-start.8 = (bf16[24,128,256]{2,1,0:T(8,128)(2,1)S(1)}, bf16[24,128,256]{2,1,0:T(8,128)(2,1)}, u32[]{:S(2)}) copy-start(bf16[24,128,256]{2,1,0:T(8,128)(2,1)} %get-tuple-element.129.a) | copy-start | bytes 4718596
  72.8 7.7 %copy-start.9 = (bf16[512,768]{1,0:T(8,128)(2,1)S(1)}, bf16[512,768]{1,0:T(8,128)(2,1)}, u32[]{:S(2)}) copy-start(bf16[512,768]{1,0:T(8,128)(2,1)} %get-tuple-element.126.q) | copy-start | bytes 2359300
  72.9 7.7 %copy-start.10 = (bf16[512,768]{1,0:T(8,128)(2,1)S(1)}, bf16[512,768]{1,0:T(8,128)(2,1)}, u32[]{:S(2)}) copy-start(bf16[512,768]{1,0:T(8,128)(2,1)} %get-tuple-element.127.k) | copy-start | bytes 2359300
  72.9 7.6 %copy-start.11 = (bf16[512,768]{1,0:T(8,128)(2,1)S(1)}, bf16[512,768]{1,0:T(8,128)(2,1)}, u32[]{:S(2)}) copy-start(bf16[512,768]{1,0:T(8,128)(2,1)} %get-tuple-element.128.v) | copy-start | bytes 2359300
  78.5 20.3 %collective-permute-start.16 = (bf16[2,2,192,384]{3,2,1,0:T(8,128)(2,1)}, bf16[2,2,192,384]{3,2,1,0:T(8,128)(2,1)}, u32[]{:S(2)}, u32[]{:S(2)}) collective-permute-start(bf16[2,2,192,384]{3,2,1,0:T(8,128)(2,1)} %get-tuple-element.142), channel_id=1, source_target_pairs={{0,16},{8,24},{16,0},{24,8},{1,17},{9,25},{17,1},{25,9},{2,18},{10... | collective-permute-start | bytes 1769480 | tf_op jit(solution)/shard_map/ppermute | solution.py:1022
  79.9 20.4 %collective-permute-start.17 = (bf16[2,2,192,384]{3,2,1,0:T(8,128)(2,1)}, bf16[2,2,192,384]{3,2,1,0:T(8,128)(2,1)}, u32[]{:S(2)}, u32[]{:S(2)}) collective-permute-start(bf16[2,2,192,384]{3,2,1,0:T(8,128)(2,1)} %get-tuple-element.144), channel_id=1, source_target_pairs={{0,1},{1,0},{2,3},{3,2},{4,5},{5,4},{6,7},{7,6},{8,9},{9,8},{10,11... | collective-permute-start | bytes 1769480 | tf_op jit(solution)/shard_map/ppermute | solution.py:1022
  90.1 11.8 %collective-permute-start.14 = (bf16[132,8,192]{2,1,0:T(8,128)(2,1)S(1)}, bf16[132,8,192]{2,1,0:T(8,128)(2,1)S(1)}, u32[]{:S(2)}, u32[]{:S(2)}) collective-permute-start(bf16[132,8,192]{2,1,0:T(8,128)(2,1)S(1)} %get-tuple-element.140.refs_4_), channel_id=1, source_target_pairs={{0,8},{8,0},{16,24},{24,16},{1,9},{9,1},{17,25},{25,17},{2,10},{10... | collective-permute-start | bytes 1216520 | tf_op jit(solution)/shard_map/ppermute | solution.py:1022
  90.2 11.7 %collective-permute-start.15 = (bf16[64,1152]{1,0:T(8,128)(2,1)S(1)}, bf16[64,1152]{1,0:T(8,128)(2,1)S(1)}, u32[]{:S(2)}, u32[]{:S(2)}) collective-permute-start(bf16[64,1152]{1,0:T(8,128)(2,1)S(1)} %get-tuple-element.141.refs_3_), channel_id=1, source_target_pairs={{0,4},{1,5},{2,6},{3,7},{4,0},{5,1},{6,2},{7,3},{8,12},{9,13},{10,... | collective-permute-start | bytes 442376 | tf_op jit(solution)/shard_map/ppermute | solution.py:1022
  90.3 16.6 %collective-permute-start.23 = (bf16[528,2304]{1,0:T(8,128)(2,1)}, bf16[528,2304]{1,0:T(8,128)(2,1)}, u32[]{:S(2)}, u32[]{:S(2)}) collective-permute-start(bf16[528,2304]{1,0:T(8,128)(2,1)} %attention_back.1.rest_0_.refs_4_), channel_id=1, source_target_pairs={{0,8},{8,0},{16,24},{24,16},{1,9},{9,1},{17,25},{25,17},{2,10},{10... | collective-permute-start | bytes 7299080 | tf_op jit(solution)/shard_map/ppermute | solution.py:1022
  90.7 2.1 %copy-start.2 = (bf16[512,3840]{1,0:T(8,128)(2,1)S(1)}, bf16[512,3840]{1,0:T(8,128)(2,1)}, u32[]{:S(2)}) copy-start(bf16[512,3840]{1,0:T(8,128)(2,1)} %get-tuple-element.145.refs_2_) | copy-start | bytes 11796484
  98.8 37.0 %collective-permute-start.20 = (bf16[2,4,192,384]{3,2,1,0:T(8,128)(2,1)}, bf16[2,4,192,384]{3,2,1,0:T(8,128)(2,1)}, u32[]{:S(2)}, u32[]{:S(2)}) collective-permute-start(bf16[2,4,192,384]{3,2,1,0:T(8,128)(2,1)} %get-tuple-element.150), channel_id=1, source_target_pairs={{0,16},{8,24},{16,0},{24,8},{1,17},{9,25},{17,1},{25,9},{2,18},{10... | collective-permute-start | bytes 3538952 | tf_op jit(solution)/shard_map/ppermute | solution.py:1022
  101.9 5.0 %copy-start.1 = (bf16[7,512,384]{2,1,0:T(8,128)(2,1)S(1)}, bf16[7,512,384]{2,1,0:T(8,128)(2,1)}, u32[]{:S(2)}) copy-start(bf16[7,512,384]{2,1,0:T(8,128)(2,1)} %get-tuple-element.135.refs_2_.refs_0_) | copy-start | bytes 8257540
  104.3 31.5 %collective-permute-start.19 = (bf16[960,384]{1,0:T(8,128)(2,1)S(1)}, bf16[960,384]{1,0:T(8,128)(2,1)S(1)}, u32[]{:S(2)}, u32[]{:S(2)}) collective-permute-start(bf16[960,384]{1,0:T(8,128)(2,1)S(1)} %get-tuple-element.149), channel_id=1, source_target_pairs={{0,1},{1,0},{2,3},{3,2},{4,5},{5,4},{6,7},{7,6},{8,9},{9,8},{10,11... | collective-permute-start | bytes 2211848 | tf_op jit(solution)/shard_map/ppermute | solution.py:1022
  104.9 24.1 %collective-permute-start.21 = (bf16[2,192,384]{2,1,0:T(8,128)(2,1)S(1)}, bf16[2,192,384]{2,1,0:T(8,128)(2,1)S(1)}, u32[]{:S(2)}, u32[]{:S(2)}) collective-permute-start(bf16[2,192,384]{2,1,0:T(8,128)(2,1)S(1)} %get-tuple-element.147.refs_5_), channel_id=1, source_target_pairs={{0,1},{1,0},{2,3},{3,2},{4,5},{5,4},{6,7},{7,6},{8,9},{9,8},{10,11... | collective-permute-start | bytes 884744 | tf_op jit(solution)/shard_map/ppermute | solution.py:1022
  106.4 27.8 %collective-permute-start.22 = (bf16[2,192,384]{2,1,0:T(8,128)(2,1)S(1)}, bf16[2,192,384]{2,1,0:T(8,128)(2,1)S(1)}, u32[]{:S(2)}, u32[]{:S(2)}) collective-permute-start(bf16[2,192,384]{2,1,0:T(8,128)(2,1)S(1)} %get-tuple-element.153), channel_id=1, source_target_pairs={{0,16},{8,24},{16,0},{24,8},{1,17},{9,25},{17,1},{25,9},{2,18},{10... | collective-permute-start | bytes 884744 | tf_op jit(solution)/shard_map/ppermute | solution.py:1022
  106.9 2.1 %copy-start.3 = (bf16[512,3840]{1,0:T(8,128)(2,1)S(1)}, bf16[512,3840]{1,0:T(8,128)(2,1)}, u32[]{:S(2)}) copy-start(bf16[512,3840]{1,0:T(8,128)(2,1)} %get-tuple-element.145.refs_2_) | copy-start | bytes 11796484
  117.8 32.2 %collective-permute-start.25 = (bf16[2,2,208,384]{3,2,1,0:T(8,128)(2,1)}, bf16[2,2,208,384]{3,2,1,0:T(8,128)(2,1)}, u32[]{:S(2)}, u32[]{:S(2)}) collective-permute-start(bf16[2,2,208,384]{3,2,1,0:T(8,128)(2,1)} %get-tuple-element.162), channel_id=1, source_target_pairs={{0,16},{8,24},{16,0},{24,8},{1,17},{9,25},{17,1},{25,9},{2,18},{10... | collective-permute-start | bytes 1916936 | tf_op jit(solution)/shard_map/ppermute | solution.py:1022
  128.9 21.1 %collective-permute-start.26 = (bf16[2,2,208,384]{3,2,1,0:T(8,128)(2,1)}, bf16[2,2,208,384]{3,2,1,0:T(8,128)(2,1)}, u32[]{:S(2)}, u32[]{:S(2)}) collective-permute-start(bf16[2,2,208,384]{3,2,1,0:T(8,128)(2,1)} %get-tuple-element.164), channel_id=1, source_target_pairs={{0,1},{1,0},{2,3},{3,2},{4,5},{5,4},{6,7},{7,6},{8,9},{9,8},{10,11... | collective-permute-start | bytes 1916936 | tf_op jit(solution)/shard_map/ppermute | solution.py:1022
  135.3 6.5 %copy-start.7 = (s32[2,4]{1,0:T(2,128)S(1)}, s32[2,4]{1,0:T(2,128)}, u32[]{:S(2)}) copy-start(s32[2,4]{1,0:T(2,128)} %len_ref.3) | copy-start | bytes 100
  135.3 19.9 %collective-permute-start.30 = (bf16[768,384]{1,0:T(8,128)(2,1)}, bf16[768,384]{1,0:T(8,128)(2,1)}, u32[]{:S(2)}, u32[]{:S(2)}) collective-permute-start(bf16[768,384]{1,0:T(8,128)(2,1)} %get-tuple-element.156.refs_2_), channel_id=1, source_target_pairs={{0,2},{1,3},{2,0},{3,1},{4,6},{5,7},{6,4},{7,5},{8,10},{9,11},{10,... | collective-permute-start | bytes 1769480 | tf_op jit(solution)/shard_map/ppermute | solution.py:1022
  138.1 26.0 %collective-permute-start.24 = (bf16[4,192,384]{2,1,0:T(8,128)(2,1)}, bf16[4,192,384]{2,1,0:T(8,128)(2,1)}, u32[]{:S(2)}, u32[]{:S(2)}) collective-permute-start(bf16[4,192,384]{2,1,0:T(8,128)(2,1)} %get-tuple-element.157.rest_0_), channel_id=1, source_target_pairs={{0,1},{1,0},{2,3},{3,2},{4,5},{5,4},{6,7},{7,6},{8,9},{9,8},{10,11... | collective-permute-start | bytes 1769480 | tf_op jit(solution)/shard_map/ppermute | solution.py:1022
  140.3 18.6 %collective-permute-start.29 = (bf16[576,384]{1,0:T(8,128)(2,1)}, bf16[576,384]{1,0:T(8,128)(2,1)}, u32[]{:S(2)}, u32[]{:S(2)}) collective-permute-start(bf16[576,384]{1,0:T(8,128)(2,1)} %get-tuple-element.158.rest_2_), channel_id=1, source_target_pairs={{0,2},{1,3},{2,0},{3,1},{4,6},{5,7},{6,4},{7,5},{8,10},{9,11},{10,... | collective-permute-start | bytes 1327112 | tf_op jit(solution)/shard_map/ppermute | solution.py:1022
  150.0 1.4 copy-start.4
  153.0 11.0 %collective-permute-start.27 = (bf16[2,208,384]{2,1,0:T(8,128)(2,1)S(1)}, bf16[2,208,384]{2,1,0:T(8,128)(2,1)S(1)}, u32[]{:S(2)}, u32[]{:S(2)}) collective-permute-start(bf16[2,208,384]{2,1,0:T(8,128)(2,1)S(1)} %get-tuple-element.166.rest_0_), channel_id=1, source_target_pairs={{0,1},{1,0},{2,3},{3,2},{4,5},{5,4},{6,7},{7,6},{8,9},{9,8},{10,11... | collective-permute-start | bytes 958472 | tf_op jit(solution)/shard_map/ppermute | solution.py:1022
  153.7 10.3 %collective-permute-start.28 = (bf16[2,208,384]{2,1,0:T(8,128)(2,1)S(1)}, bf16[2,208,384]{2,1,0:T(8,128)(2,1)S(1)}, u32[]{:S(2)}, u32[]{:S(2)}) collective-permute-start(bf16[2,208,384]{2,1,0:T(8,128)(2,1)S(1)} %get-tuple-element.168), channel_id=1, source_target_pairs={{0,16},{8,24},{16,0},{24,8},{1,17},{9,25},{17,1},{25,9},{2,18},{10... | collective-permute-start | bytes 958472 | tf_op jit(solution)/shard_map/ppermute | solution.py:1022
  160.2 28.9 %collective-permute-start.33 = (bf16[576,384]{1,0:T(8,128)(2,1)S(1)}, bf16[576,384]{1,0:T(8,128)(2,1)S(1)}, u32[]{:S(2)}, u32[]{:S(2)}) collective-permute-start(bf16[576,384]{1,0:T(8,128)(2,1)S(1)} %get-tuple-element.176), channel_id=1, source_target_pairs={{0,4},{1,5},{2,6},{3,7},{4,0},{5,1},{6,2},{7,3},{8,12},{9,13},{10,... | collective-permute-start | bytes 1327112 | tf_op jit(solution)/shard_map/ppermute | solution.py:1022
  165.8 23.4 %collective-permute-start.32 = (bf16[2,208,384]{2,1,0:T(8,128)(2,1)S(1)}, bf16[2,208,384]{2,1,0:T(8,128)(2,1)S(1)}, u32[]{:S(2)}, u32[]{:S(2)}) collective-permute-start(bf16[2,208,384]{2,1,0:T(8,128)(2,1)S(1)} %get-tuple-element.175), channel_id=1, source_target_pairs={{0,2},{1,3},{2,0},{3,1},{4,6},{5,7},{6,4},{7,5},{8,10},{9,11},{10,... | collective-permute-start | bytes 958472 | tf_op jit(solution)/shard_map/ppermute | solution.py:1022
  166.7 22.5 %collective-permute-start.31 = (bf16[2,192,384]{2,1,0:T(8,128)(2,1)S(1)}, bf16[2,192,384]{2,1,0:T(8,128)(2,1)S(1)}, u32[]{:S(2)}, u32[]{:S(2)}) collective-permute-start(bf16[2,192,384]{2,1,0:T(8,128)(2,1)S(1)} %get-tuple-element.173.rest_0_), channel_id=1, source_target_pairs={{0,2},{1,3},{2,0},{3,1},{4,6},{5,7},{6,4},{7,5},{8,10},{9,11},{10,... | collective-permute-start | bytes 884744 | tf_op jit(solution)/shard_map/ppermute | solution.py:1022
  189.3 13.6 %collective-permute-start.34 = (bf16[400,384]{1,0:T(8,128)(2,1)S(1)}, bf16[400,384]{1,0:T(8,128)(2,1)S(1)}, u32[]{:S(2)}, u32[]{:S(2)}) collective-permute-start(bf16[400,384]{1,0:T(8,128)(2,1)S(1)} %get-tuple-element.178.refs_4_), channel_id=1, source_target_pairs={{0,4},{1,5},{2,6},{3,7},{4,0},{5,1},{6,2},{7,3},{8,12},{9,13},{10,... | collective-permute-start | bytes 921608 | tf_op jit(solution)/shard_map/ppermute | solution.py:1022
where the time goes:
time: 206 us; the launch traced here: 205 us
  Pallas kernels  100 us (49%)
  waiting for transfers between devices  62.2 us (30%)
  starting transfers between devices  33.6 us (16%)
  local copies, waits for them, and re-layouts  7.85 us (4%)
    ppermute x34, waiting for transfers between devices, flip(): lax.ppermute(values, axis, [(i, i ^ bits) for i in range(lax.axis_size(ax...  60.2 us
    pallas_call x18, Pallas kernels, call(): pl.pallas_call(functools.partial(kernel), out_shape=list(outs), name=name...  55.3 us
    ppermute x34, starting transfers between devices, flip(): lax.ppermute(values, axis, [(i, i ^ bits) for i in range(lax.axis_size(ax...  33.1 us
    pallas_call x1, Pallas kernels, forward(): pl.pallas_call(functools.partial(fwd_kernel, cut), out_shape=outs, out_sp...  24.3 us
    pallas_call x1, Pallas kernels, top(): pl.pallas_call(functools.partial(top_kernel, cut, S // 2, len(gathered),...  20.9 us
    unnamed x29, local copies, waits for them, and re-layouts  7.21 us
  transfers between devices with their start and end apart: 35, of which 13 were waited for; matrix products, arithmetic and copies ran while one was open for 1% of the time, Pallas kernels for 26%

commit v1 on v0

--- a/solution.py
+++ b/solution.py
@@ -1177,6 +1177,11 @@
     expand_out[1] = e1[...]
 
 
+def finish_kernel(wa, own1, own2, got12, own34, got34, r1, e1, reduce_out, expand_out, *outs):
+    finish_wide_kernel(own2, got12, own34, got34, r1, e1, reduce_out, expand_out)
+    finish_attend_kernel(wa, own34, got34, own1, got12, *outs)
+
+
 def finish_attend_kernel(wa, own34, got34, own1, got12, *outs):
     attend_out, output_out, bias_out, gains_out, wb_out, pb_out = outs
     kr = own1.shape[0]
@@ -1239,32 +1244,30 @@
         gp = attend_back(gc, q, k, v, a, vectors, (ch2[0],))
         gps = twin(gp[0])
         packed, left = pack(stay, got_y, left, cross(left, "x"), (gp[0],))
-        ch3 = widen_weight_back(cut, acts, gfs, (packed,))
+        t = s2.fold(packed)
+        ch3 = widen_weight_back(cut, acts, gfs, (t,))
         s3 = Share(ch3, MODE[3])
-        t = s2.fold(ch3[0])
-        ch1 = top_weights(cut, [stay, got_y, flip(packed, "gx", 1)], (left, flip(left, "gy", 4)), (t,))
+        ch1 = top_weights(cut, [stay, got_y, flip(packed, "gx", 1)], (left, flip(left, "gy", 4)), (ch3[0], *s2.got))
         got1 = cross(ch1[1], "x")
-        ch4 = attend_weight(cut, acts, gfs, [[t] for t in gps], (ch1[0],))
-        keep2, got2, t = s2.spread(ch1[2], ch4[0])
+        keep2, got2, t = s2.spread(ch1[2], ch1[0])
         left = [ch1[2], got2]
-        t = s3.fold(t, got1)
+        ch4 = attend_weight(cut, acts, gfs, [[t] for t in gps], (t,))
         s4 = Share(ch4, MODE[4])
         kr, dn, dv = D // GX, D // GY, D // n
-        keep1, got1, t = spread_rows(ch1[0], got1, kr, (t,))
-        gx0, sc0 = input_back(n * PH, lengths, tot, gz1, gp, wqkv, (t,))
+        keep1, got1, t = spread_rows(ch1[0], got1, kr, (ch4[0],))
+        t = s3.fold(t, got2)
+        own1, rows1, own2, got12 = settle_two(keep1, got1, keep2, got2, kr, (t,))
+        gx0, sc0 = input_back(n * PH, lengths, tot, gz1, gp, wqkv, (rows1,))
         t = s4.fold(gx0)
-        own1, rows1, own2, got12 = settle_two(keep1, got1, keep2, got2, kr, (t,))
-        last, t = spread_two(s3, s4, (rows1,))
-        own34, got34, t = settle_last(last, (t, got12))
+        last, t = spread_two(s3, s4, (t, got12))
+        own34, got34, t = settle_last(last, (t,))
         d_pool, d_expand1, d_reduce1 = row_weights(cut, left, [rows1, got12], (t,))
-        d_reduce, d_expand = call(
-            finish_wide_kernel, "finish_wide", 16, [sds((2, dn, FF // GX), F32), sds((2, kr, FF // GY), F32)],
-            (own2, got12, own34, got34, d_reduce1, d_expand1))
+        d_reduce, d_expand, d_attend, d_output, d_bias, d_gains, d_wb, d_pb = call(
+            functools.partial(finish_kernel, wa), "finish", 24,
+            [sds((2, dn, FF // GX), F32), sds((2, kr, FF // GY), F32), sds((2, kr, wa), F32), sds((2, kr, dn), F32),
+             sds((6, 2, dv), F32), sds((2, 2, dv), F32), sds((2, FF // n), F32), sds((1, dv), F32)],
+            (own1, own2, got12, own34, got34, d_reduce1, d_expand1))
         d_reduce = d_reduce.transpose(0, 2, 1)
-        d_attend, d_output, d_bias, d_gains, d_wb, d_pb = call(
-            functools.partial(finish_attend_kernel, wa), "finish_attend", 16,
-            [sds((2, kr, wa), F32), sds((2, kr, dn), F32), sds((6, 2, dv), F32), sds((2, 2, dv), F32),
-             sds((2, FF // n), F32), sds((1, dv), F32)], (own34, got34, own1, got12))
         d_bias, d_pb = d_bias.transpose(1, 0, 2), d_pb.reshape(dv)
     else:
         ch2 = narrow_weight(cut, gys, acts)

time: 206 us -> 194 us (0.942)
  waiting for transfers between devices: 62.2 us -> 56.9 us
  Pallas kernels: 100 us -> 96.5 us
    pallas_call x18 -> x17, Pallas kernels: 55.3 us -> 51.3 us  [call(): pl.pallas_call(functools.partial(kernel), out_shape=list(outs), name=name...]
    ppermute x34, waiting for transfers between devices: 60.2 us -> 56.9 us  [flip(): lax.ppermute(values, axis, [(i, i ^ bits) for i in range(lax.axis_size(ax...]
    ppermute x34, starting transfers between devices: 33.1 us -> 30.3 us  [flip(): lax.ppermute(values, axis, [(i, i ^ bits) for i in range(lax.axis_size(ax...]
    unnamed x29 -> x33, local copies, waits for them, and re-layouts: 7.21 us -> 6.85 us
  transfers between devices with their start and end apart: 35 -> 35, of which waited for: 13 -> 15; matrix products, arithmetic and copies ran while one was open for 1% -> 1% of each run, Pallas kernels for 26% -> 24%
where the time goes in v1:
time: 194 us
  Pallas kernels  96.5 us (50%)
  waiting for transfers between devices  56.9 us (29%)
  starting transfers between devices  31.7 us (16%)
  local copies, waits for them, and re-layouts  7.5 us (4%)
    ppermute x34, waiting for transfers between devices, flip(): lax.ppermute(values, axis, [(i, i ^ bits) for i in range(lax.axis_size(ax...  56.9 us
    pallas_call x17, Pallas kernels, call(): pl.pallas_call(functools.partial(kernel), out_shape=list(outs), name=name...  51.3 us
    ppermute x34, starting transfers between devices, flip(): lax.ppermute(values, axis, [(i, i ^ bits) for i in range(lax.axis_size(ax...  30.3 us
    pallas_call x1, Pallas kernels, forward(): pl.pallas_call(functools.partial(fwd_kernel, cut), out_shape=outs, out_sp...  24.3 us
    pallas_call x1, Pallas kernels, top(): pl.pallas_call(functools.partial(top_kernel, cut, S // 2, len(gathered),...  20.9 us
    unnamed x33, local copies, waits for them, and re-layouts  6.85 us
  transfers between devices with their start and end apart: 35, of which 15 were waited for; matrix products, arithmetic and copies ran while one was open for 1% of the time, Pallas kernels for 24%

profile of v1, /device:TPU:0, one launch (start us, length us, event | category | flops | bytes accessed | tf_op | source)
XLA Modules:
  0.0 193.5 jit_solution(12845235514440540242)
XLA Ops:
  0.7 24.3 %encode.1 = (bf16[512,768]{1,0:T(8,128)(2,1)}, bf16[512,768]{1,0:T(8,128)(2,1)}, bf16[512,768]{1,0:T(8,128)(2,1)}, bf16[24,128,256]{2,1,0:T(8,128)(2,1)}, bf16[5...) custom-call(s32[2,4]{1,0:T(2,128)} %len_ref.3, ...), custom_call_target="tpu_custom_call" | custom-call | tf_op jit(solution)/shard_map/encode/pallas_call | solution.py:310
  25.5 4.7 %collective-permute-start.2 = (bf16[8,896]{1,0:T(8,128)(2,1)}, bf16[8,896]{1,0:T(8,128)(2,1)S(1)}, u32[]{:S(2)}, u32[]{:S(2)}) collective-permute-start(bf16[8,896]{1,0:T(8,128)(2,1)} %get-tuple-element.102.refs_0_), channel_id=1, source_target_pairs={{0,6},{1,7},{2,4},{3,5},{4,2},{5,3},{6,0},{7,1},{8,14},{9,15},{10,... | collective-permute-start | bytes 43016 | tf_op jit(solution)/shard_map/ppermute | solution.py:1022
  31.6 2.5 %collective-permute-done = bf16[8,896]{1,0:T(8,128)(2,1)S(1)} collective-permute-done((bf16[8,896]{1,0:T(8,128)(2,1)}, bf16[8,896]{1,0:T(8,128)(2,1)S(1)}, u32[]{:S(2)}, u32[]{:S(2)}) %collective-permute-start) | collective-permute-done | bytes 14368 | tf_op jit(solution)/shard_map/ppermute | solution.py:1022
  34.1 0.9 collective-permute-done.1
  35.0 1.6 collective-permute-start.3
  36.6 1.5 collective-permute-start.5
  38.6 1.0 collective-permute-done.3
  39.6 2.6 %collective-permute-done.4 = bf16[32,896]{1,0:T(8,128)(2,1)S(1)} collective-permute-done((bf16[32,896]{1,0:T(8,128)(2,1)S(1)}, bf16[32,896]{1,0:T(8,128)(2,1)S(1)}, u32[]{:S(2)}, u32[]{:S(2)}) %collective-permute-start.4) | collective-permute-done | bytes 57376 | tf_op jit(solution)/shard_map/ppermute | solution.py:1022
  42.4 1.2 collective-permute-start.7
  44.6 1.8 collective-permute-done.7.refs_23_
  47.8 20.9 %rank_and_top_back.1 = (bf16[32,1152]{1,0:T(8,128)(2,1)}, f32[8,128]{1,0:T(8,128)S(1)}, f32[8,128]{1,0:T(8,128)S(1)}, bf16[512,768]{1,0:T(8,128)(2,1)S(1)}, f32[...) custom-call(f32[2,2,768]{2,1,0:T(2,128)S(1)} %copy-done.7, ...), custom_call_target="tpu_custom_call" | custom-call | bytes 1 | tf_op jit(solution)/shard_map/rank_and_top_back/pallas_call | solution.py:622
  69.1 1.0 collective-permute-start.13
  70.1 1.4 collective-permute-start.12
  71.6 5.6 %narrowing_weight.1 = (bf16[2,2,192,384]{3,2,1,0:T(8,128)(2,1)S(1)}, bf16[2,2,192,384]{3,2,1,0:T(8,128)(2,1)}, bf16[2,2,192,384]{3,2,1,0:T(8,128)(2,1)S(1)}, bf16[2,2,192,384]{3,2,1,0:T(8,128)(2,1)}) custom-call(bf16[512,768]{1,0:T(8,128)(2,1)S(1)} %get-tuple-element.134.refs_0_, bf16[512,768]{1,0:T(8,128)(2,1)S(1)} %collective-permute-done.11.refs_1_, ...), custom_call_target="tpu_custom_call" | custom-call | bytes 1 | tf_op jit(solution)/shard_map/narrowing_weight/pallas_call | solution.py:594
  77.8 1.3 collective-permute-start.18
  79.1 8.5 %attention_back.1.rest_0_.refs_4_ = bf16[528,2304]{1,0:T(8,128)(2,1)} custom-call(bf16[512,768]{1,0:T(8,128)(2,1)S(1)} %get-tuple-element.125.gc, bf16[512,768]{1,0:T(8,128)(2,1)S(1)} %copy-done.11, bf16[512,768]{1,0:T(8,128)(2,1)S(1)} %copy-done.12, bf16[512,768]{1,0:T(8,128)(2,1)S(1)} %copy-done.13, bf16[24,128,256]{2,1,0:T(8,128)(2,1)S(1)} %copy-done.10, ...), custom_call_target="tpu_custom_call" | custom-call | flops 9999999827968 | bytes 1 | tf_op jit(solution)/shard_map/attention_back/pallas_call | solution.py:594
  87.6 1.2 pack.1
  88.9 4.7 %collective-permute-done.17.refs_1_ = bf16[2,2,192,384]{3,2,1,0:T(8,128)(2,1)} collective-permute-done((bf16[2,2,192,384]{3,2,1,0:T(8,128)(2,1)}, bf16[2,2,192,384]{3,2,1,0:T(8,128)(2,1)}, u32[]{:S(2)}, u32[]{:S(2)}) %collective-permute-start.17) | collective-permute-done | bytes 589856 | tf_op jit(solution)/shard_map/ppermute | solution.py:1022
  93.6 1.5 fold.3
  95.1 1.5 collective-permute-start.20
  97.2 2.1 %collective-permute-start.15 = (bf16[64,1152]{1,0:T(8,128)(2,1)S(1)}, bf16[64,1152]{1,0:T(8,128)(2,1)S(1)}, u32[]{:S(2)}, u32[]{:S(2)}) collective-permute-start(bf16[64,1152]{1,0:T(8,128)(2,1)S(1)} %get-tuple-element.141.refs_3_), channel_id=1, source_target_pairs={{0,4},{1,5},{2,6},{3,7},{4,0},{5,1},{6,2},{7,3},{8,12},{9,13},{10,... | collective-permute-start | bytes 442376 | tf_op jit(solution)/shard_map/ppermute | solution.py:1022
  99.2 5.0 %widening_weight.1 = (bf16[2,4,192,384]{3,2,1,0:T(8,128)(2,1)S(1)}, bf16[2,4,192,384]{3,2,1,0:T(8,128)(2,1)S(1)}) custom-call(bf16[7,512,384]{2,1,0:T(8,128)(2,1)S(1)} %copy-done, bf16[7,512,384]{2,1,0:T(8,128)(2,1)S(1)} %collective-permute-done.10.refs_26_.refs_3_.refs_1_, bf16[512,3840]{1,0:T(8,128)(2,1)S(1)} %copy-done.2, ...), custom_call_target="tpu_custom_call" | custom-call | bytes 1 | tf_op jit(solution)/shard_map/widening_weight/pallas_call | solution.py:594
  104.2 1.1 collective-permute-done.15.refs_4_
  105.4 2.2 %top_weights.1 = (bf16[960,384]{1,0:T(8,128)(2,1)S(1)}, bf16[960,384]{1,0:T(8,128)(2,1)S(1)}, bf16[128,1152]{1,0:T(8,128)(2,1)S(1)}) custom-call(bf16[92,8,192]{2,1,0:T(8,128)(2,1)S(1)} %get-tuple-element.137.stay.refs_0_, bf16[92,8,192]{2,1,0:T(8,128)(2,1)} %collective-permute-done.12.got.refs_1_, bf16[132,8,192]{2,1,0:T(8,128)(2,1)S(1)} %collective-permute-done.14.refs_2_, ...), custom_call_target="tpu_custom_call" | custom-call | flops 9999999827968 | bytes 1 | tf_op jit(solution)/shard_map/top_weights/pallas_call | solution.py:594
  107.7 1.3 collective-permute-start.21
  108.9 1.1 collective-permute-start.25
  110.5 1.8 copy-done.1
  112.2 2.1 %copy-done.3 = bf16[512,3840]{1,0:T(8,128)(2,1)S(1)} copy-done((bf16[512,3840]{1,0:T(8,128)(2,1)S(1)}, bf16[512,3840]{1,0:T(8,128)(2,1)}, u32[]{:S(2)}) %copy-start.3) | copy-done | bytes 3932184
  114.3 8.8 %attention_weight.1 = (bf16[2,2,208,384]{3,2,1,0:T(8,128)(2,1)S(1)}, bf16[2,2,208,384]{3,2,1,0:T(8,128)(2,1)}, bf16[2,2,208,384]{3,2,1,0:T(8,128)(2,1)S(1)}, bf16[2,2,208,384]{3,2,1,0:T(8,128)(2,1)}) custom-call(bf16[7,512,384]{2,1,0:T(8,128)(2,1)S(1)} %copy-done.1, bf16[7,512,384]{2,1,0:T(8,128)(2,1)S(1)} %collective-permute-done.10.refs_26_.refs_3_.refs_1_, ...), custom_call_target="tpu_custom_call" | custom-call | bytes 1 | tf_op jit(solution)/shard_map/attention_weight/pallas_call | solution.py:594
  123.1 2.7 %collective-permute-done.21.got = bf16[960,384]{1,0:T(8,128)(2,1)S(1)} collective-permute-done((bf16[960,384]{1,0:T(8,128)(2,1)S(1)}, bf16[960,384]{1,0:T(8,128)(2,1)S(1)}, u32[]{:S(2)}, u32[]{:S(2)}) %collective-permute-start.21) | collective-permute-done | bytes 737312 | tf_op jit(solution)/shard_map/ppermute | solution.py:1022
  126.0 0.9 collective-permute-start.28
  127.0 1.7 collective-permute-start.29
  128.7 9.2 %collective-permute-done.25.refs_1_ = bf16[2,4,192,384]{3,2,1,0:T(8,128)(2,1)S(1)} collective-permute-done((bf16[2,4,192,384]{3,2,1,0:T(8,128)(2,1)S(1)}, bf16[2,4,192,384]{3,2,1,0:T(8,128)(2,1)S(1)}, u32[]{:S(2)}, u32[]{:S(2)}) %collective-permute-start.25) | collective-permute-done | bytes 1179680 | tf_op jit(solution)/shard_map/ppermute | solution.py:1022
  137.9 1.0 fold.4
  140.5 1.3 collective-permute-start.26
  141.7 8.2 %input_back.1 = (f32[512,768]{1,0:T(8,128)}, f32[512,768]{1,0:T(8,128)}) custom-call(s32[2,4]{1,0:T(2,128)S(1)} %copy-done.9, f32[8,128]{1,0:T(8,128)S(1)} %get-tuple-element.123.tot_ref, f32[512,768]{1,0:T(8,128)S(1)} %get-tuple-element.124.gz_ref, bf16[528,2304]{1,0:T(8,128)(2,1)} %attention_back.1.rest_0_.refs_4_, bf16[2,768,2304]{2,1,0:T(8,128)(2,1)} %rest_1_.1, ...), custom_call_target="tpu_custom_call" | custom-call | flops 9999999827968 | bytes 1 | tf_op jit(solution)/shard_map/input_back/pallas_call | solution.py:594
  150.0 1.4 copy-done.4
  151.4 1.6 fold.5
  153.0 1.5 collective-permute-start.31
  154.8 6.1 %collective-permute-done.31.refs_5_ = bf16[2,208,384]{2,1,0:T(8,128)(2,1)S(1)} collective-permute-done((bf16[2,208,384]{2,1,0:T(8,128)(2,1)S(1)}, bf16[2,208,384]{2,1,0:T(8,128)(2,1)S(1)}, u32[]{:S(2)}, u32[]{:S(2)}) %collective-permute-start.31) | collective-permute-done | bytes 319520 | tf_op jit(solution)/shard_map/ppermute | solution.py:1022
  161.0 1.5 collective-permute-done.30.refs_3_
  162.4 1.7 spread_two.1
  164.2 1.1 collective-permute-start.33
  165.2 1.0 collective-permute-start.32
  166.2 11.4 %collective-permute-done.32.got3 = bf16[2,192,384]{2,1,0:T(8,128)(2,1)S(1)} collective-permute-done((bf16[2,192,384]{2,1,0:T(8,128)(2,1)S(1)}, bf16[2,192,384]{2,1,0:T(8,128)(2,1)S(1)}, u32[]{:S(2)}, u32[]{:S(2)}) %collective-permute-start.32) | collective-permute-done | bytes 294944 | tf_op jit(solution)/shard_map/ppermute | solution.py:1022
  178.5 2.1 %row_weights.1 = (f32[192,96]{1,0:T(8,128)}, f32[192,384]{1,0:T(8,128)S(1)}, f32[96,768]{1,0:T(8,128)S(1)}) custom-call(bf16[128,1152]{1,0:T(8,128)(2,1)S(1)} %copy-done.6, bf16[768,384]{1,0:T(8,128)(2,1)S(1)} %collective-permute-done.24.refs_3_.got2.refs_1_, bf16[192,384]{1,0:T(8,128)(2,1)S(1)} %get-tuple-element.161.rest_2_.refs_2_, ...), custom_call_target="tpu_custom_call" | custom-call | bytes 1 | tf_op jit(solution)/shard_map/row_weights/pallas_call | solution.py:594
  180.7 10.5 %collective-permute-done.34.got34 = bf16[400,384]{1,0:T(8,128)(2,1)S(1)} collective-permute-done((bf16[400,384]{1,0:T(8,128)(2,1)S(1)}, bf16[400,384]{1,0:T(8,128)(2,1)S(1)}, u32[]{:S(2)}, u32[]{:S(2)}) %collective-permute-start.34) | collective-permute-done | bytes 307232 | tf_op jit(solution)/shard_map/ppermute | solution.py:1022
  191.1 2.4 %finish.1 = (f32[2,96,768]{2,1,0:T(8,128)}, f32[2,192,384]{2,1,0:T(8,128)}, f32[2,192,288]{2,1,0:T(8,128)}, f32[2,192,96]{2,1,0:T(8,128)}, f32[6,2,24]{2,1,0:T(2...) custom-call(f32[192,384]{1,0:T(8,128)S(1)} %get-tuple-element.164.own1, ...), custom_call_target="tpu_custom_call" | custom-call | bytes 1 | tf_op jit(solution)/shard_map/finish/pallas_call | solution.py:594
  (77 shorter events, 10.3 us)
Async XLA Ops:
  0.6 46.5 %copy-start.7 = (f32[2,2,768]{2,1,0:T(2,128)S(1)}, f32[2,2,768]{2,1,0:T(2,128)}, u32[]{:S(2)}) copy-start(f32[2,2,768]{2,1,0:T(2,128)} %gain_ref.3) | copy-start | bytes 36868
  25.0 22.1 %collective-permute-start.10 = (bf16[7,512,384]{2,1,0:T(8,128)(2,1)}, bf16[7,512,384]{2,1,0:T(8,128)(2,1)S(1)}, u32[]{:S(2)}, u32[]{:S(2)}) collective-permute-start(bf16[7,512,384]{2,1,0:T(8,128)(2,1)} %get-tuple-element.121), channel_id=1, source_target_pairs={{0,8},{8,0},{16,24},{24,16},{1,9},{9,1},{17,25},{25,17},{2,10},{10... | collective-permute-start | bytes 8257544 | tf_op jit(solution)/shard_map/ppermute | solution.py:1022
  25.5 9.5 %collective-permute-start.2 = (bf16[8,896]{1,0:T(8,128)(2,1)}, bf16[8,896]{1,0:T(8,128)(2,1)S(1)}, u32[]{:S(2)}, u32[]{:S(2)}) collective-permute-start(bf16[8,896]{1,0:T(8,128)(2,1)} %get-tuple-element.102.refs_0_), channel_id=1, source_target_pairs={{0,6},{1,7},{2,4},{3,5},{4,2},{5,3},{6,0},{7,1},{8,14},{9,15},{10,... | collective-permute-start | bytes 43016 | tf_op jit(solution)/shard_map/ppermute | solution.py:1022
  30.2 4.8 %collective-permute-start.1 = (bf16[8,896]{1,0:T(8,128)(2,1)}, bf16[8,896]{1,0:T(8,128)(2,1)S(1)}, u32[]{:S(2)}, u32[]{:S(2)}) collective-permute-start(bf16[8,896]{1,0:T(8,128)(2,1)} %get-tuple-element.102.refs_0_), channel_id=1, source_target_pairs={{0,4},{1,5},{2,6},{3,7},{4,0},{5,1},{6,2},{7,3},{8,12},{9,13},{10,... | collective-permute-start | bytes 43016 | tf_op jit(solution)/shard_map/ppermute | solution.py:1022
  30.2 3.9 %collective-permute-start = (bf16[8,896]{1,0:T(8,128)(2,1)}, bf16[8,896]{1,0:T(8,128)(2,1)S(1)}, u32[]{:S(2)}, u32[]{:S(2)}) collective-permute-start(bf16[8,896]{1,0:T(8,128)(2,1)} %get-tuple-element.102.refs_0_), channel_id=1, source_target_pairs={{0,2},{1,3},{2,0},{3,1},{4,6},{5,7},{6,4},{7,5},{8,10},{9,11},{10,... | collective-permute-start | bytes 43016 | tf_op jit(solution)/shard_map/ppermute | solution.py:1022
  35.0 4.6 %collective-permute-start.3 = (bf16[32,896]{1,0:T(8,128)(2,1)S(1)}, bf16[32,896]{1,0:T(8,128)(2,1)S(1)}, u32[]{:S(2)}, u32[]{:S(2)}) collective-permute-start(bf16[32,896]{1,0:T(8,128)(2,1)S(1)} %get-tuple-element.192), channel_id=1, source_target_pairs={{0,1},{1,0},{2,3},{3,2},{4,5},{5,4},{6,7},{7,6},{8,9},{9,8},{10,11... | collective-permute-start | bytes 172040 | tf_op jit(solution)/shard_map/ppermute | solution.py:1022
  36.6 5.7 %collective-permute-start.5 = (bf16[32,896]{1,0:T(8,128)(2,1)S(1)}, bf16[32,896]{1,0:T(8,128)(2,1)S(1)}, u32[]{:S(2)}, u32[]{:S(2)}) collective-permute-start(bf16[32,896]{1,0:T(8,128)(2,1)S(1)} %get-tuple-element.192), channel_id=1, source_target_pairs={{0,17},{1,16},{2,19},{3,18},{4,21},{5,20},{6,23},{7,22},{8,25},{9,... | collective-permute-start | bytes 172040 | tf_op jit(solution)/shard_map/ppermute | solution.py:1227
  38.1 4.2 %collective-permute-start.4 = (bf16[32,896]{1,0:T(8,128)(2,1)S(1)}, bf16[32,896]{1,0:T(8,128)(2,1)S(1)}, u32[]{:S(2)}, u32[]{:S(2)}) collective-permute-start(bf16[32,896]{1,0:T(8,128)(2,1)S(1)} %get-tuple-element.192), channel_id=1, source_target_pairs={{0,16},{8,24},{16,0},{24,8},{1,17},{9,25},{17,1},{25,9},{2,18},{10... | collective-permute-start | bytes 172040 | tf_op jit(solution)/shard_map/ppermute | solution.py:1022
  42.3 4.8 %collective-permute-start.6 = (bf16[128,896]{1,0:T(8,128)(2,1)S(1)}, bf16[128,896]{1,0:T(8,128)(2,1)S(1)}, u32[]{:S(2)}, u32[]{:S(2)}) collective-permute-start(bf16[128,896]{1,0:T(8,128)(2,1)S(1)} %constant_dynamic-update-slice_fusion.4.refs_20_), channel_id=1, source_target_pairs={{0,8},{8,0},{16,24},{24,16},{1,9},{9,1},{17,25},{25,17},{2,10},{10... | collective-permute-start | bytes 688136 | tf_op jit(solution)/shard_map/ppermute | solution.py:1022
  42.4 4.0 %collective-permute-start.7 = (bf16[8,1152]{1,0:T(8,128)(2,1)}, bf16[8,1152]{1,0:T(8,128)(2,1)S(1)}, u32[]{:S(2)}, u32[]{:S(2)}) collective-permute-start(bf16[8,1152]{1,0:T(8,128)(2,1)} %get-tuple-element.118), channel_id=1, source_target_pairs={{0,16},{8,24},{16,0},{24,8},{1,17},{9,25},{17,1},{25,9},{2,18},{10... | collective-permute-start | bytes 55304 | tf_op jit(solution)/shard_map/ppermute | solution.py:1022
  43.5 2.9 %collective-permute-start.8 = (bf16[8,1152]{1,0:T(8,128)(2,1)}, bf16[8,1152]{1,0:T(8,128)(2,1)S(1)}, u32[]{:S(2)}, u32[]{:S(2)}) collective-permute-start(bf16[8,1152]{1,0:T(8,128)(2,1)} %get-tuple-element.119), channel_id=1, source_target_pairs={{0,8},{8,0},{16,24},{24,16},{1,9},{9,1},{17,25},{25,17},{2,10},{10... | collective-permute-start | bytes 55304 | tf_op jit(solution)/shard_map/ppermute | solution.py:1022
  43.7 3.4 %collective-permute-start.9 = (bf16[8,1152]{1,0:T(8,128)(2,1)}, bf16[8,1152]{1,0:T(8,128)(2,1)S(1)}, u32[]{:S(2)}, u32[]{:S(2)}) collective-permute-start(bf16[8,1152]{1,0:T(8,128)(2,1)} %get-tuple-element.120), channel_id=1, source_target_pairs={{0,24},{8,16},{16,8},{24,0},{1,25},{9,17},{17,9},{25,1},{2,26},{10... | collective-permute-start | bytes 55304 | tf_op jit(solution)/shard_map/ppermute | solution.py:1022
  47.8 23.7 %copy-start = (bf16[7,512,384]{2,1,0:T(8,128)(2,1)S(1)}, bf16[7,512,384]{2,1,0:T(8,128)(2,1)}, u32[]{:S(2)}) copy-start(bf16[7,512,384]{2,1,0:T(8,128)(2,1)} %get-tuple-element.135.refs_2_.refs_0_) | copy-start | bytes 8257540
  68.7 2.8 %collective-permute-start.11 = (bf16[512,768]{1,0:T(8,128)(2,1)S(1)}, bf16[512,768]{1,0:T(8,128)(2,1)S(1)}, u32[]{:S(2)}, u32[]{:S(2)}) collective-permute-start(bf16[512,768]{1,0:T(8,128)(2,1)S(1)} %get-tuple-element.134.refs_0_), channel_id=1, source_target_pairs={{0,8},{8,0},{16,24},{24,16},{1,9},{9,1},{17,25},{25,17},{2,10},{10... | collective-permute-start | bytes 2359304 | tf_op jit(solution)/shard_map/ppermute | solution.py:1022
  69.1 18.5 %collective-permute-start.13 = (bf16[32,1152]{1,0:T(8,128)(2,1)}, bf16[32,1152]{1,0:T(8,128)(2,1)}, u32[]{:S(2)}, u32[]{:S(2)}) collective-permute-start(bf16[32,1152]{1,0:T(8,128)(2,1)} %get-tuple-element.139.left_a), channel_id=1, source_target_pairs={{0,1},{1,0},{2,3},{3,2},{4,5},{5,4},{6,7},{7,6},{8,9},{9,8},{10,11... | collective-permute-start | bytes 221192 | tf_op jit(solution)/shard_map/ppermute | solution.py:1022
  70.1 17.5 %collective-permute-start.12 = (bf16[92,8,192]{2,1,0:T(8,128)(2,1)}, bf16[92,8,192]{2,1,0:T(8,128)(2,1)}, u32[]{:S(2)}, u32[]{:S(2)}) collective-permute-start(bf16[92,8,192]{2,1,0:T(8,128)(2,1)} %get-tuple-element.138), channel_id=1, source_target_pairs={{0,16},{8,24},{16,0},{24,8},{1,17},{9,25},{17,1},{25,9},{2,18},{10... | collective-permute-start | bytes 847880 | tf_op jit(solution)/shard_map/ppermute | solution.py:1022
  71.5 27.7 %collective-permute-start.16 = (bf16[512,3840]{1,0:T(8,128)(2,1)}, bf16[512,3840]{1,0:T(8,128)(2,1)}, u32[]{:S(2)}, u32[]{:S(2)}) collective-permute-start(bf16[512,3840]{1,0:T(8,128)(2,1)} %get-tuple-element.142.refs_2_), channel_id=1, source_target_pairs={{0,8},{8,0},{16,24},{24,16},{1,9},{9,1},{17,25},{25,17},{2,10},{10... | collective-permute-start | bytes 11796488 | tf_op jit(solution)/shard_map/ppermute | solution.py:1022
  71.5 7.6 %copy-start.10 = (bf16[24,128,256]{2,1,0:T(8,128)(2,1)S(1)}, bf16[24,128,256]{2,1,0:T(8,128)(2,1)}, u32[]{:S(2)}) copy-start(bf16[24,128,256]{2,1,0:T(8,128)(2,1)} %get-tuple-element.129.a) | copy-start | bytes 4718596
  71.5 7.6 %copy-start.11 = (bf16[512,768]{1,0:T(8,128)(2,1)S(1)}, bf16[512,768]{1,0:T(8,128)(2,1)}, u32[]{:S(2)}) copy-start(bf16[512,768]{1,0:T(8,128)(2,1)} %get-tuple-element.126.q) | copy-start | bytes 2359300
  71.5 7.6 %copy-start.12 = (bf16[512,768]{1,0:T(8,128)(2,1)S(1)}, bf16[512,768]{1,0:T(8,128)(2,1)}, u32[]{:S(2)}) copy-start(bf16[512,768]{1,0:T(8,128)(2,1)} %get-tuple-element.127.k) | copy-start | bytes 2359300
  71.6 7.6 %copy-start.13 = (bf16[512,768]{1,0:T(8,128)(2,1)S(1)}, bf16[512,768]{1,0:T(8,128)(2,1)}, u32[]{:S(2)}) copy-start(bf16[512,768]{1,0:T(8,128)(2,1)} %get-tuple-element.128.v) | copy-start | bytes 2359300
  77.2 16.4 %collective-permute-start.17 = (bf16[2,2,192,384]{3,2,1,0:T(8,128)(2,1)}, bf16[2,2,192,384]{3,2,1,0:T(8,128)(2,1)}, u32[]{:S(2)}, u32[]{:S(2)}) collective-permute-start(bf16[2,2,192,384]{3,2,1,0:T(8,128)(2,1)} %get-tuple-element.143), channel_id=1, source_target_pairs={{0,16},{8,24},{16,0},{24,8},{1,17},{9,25},{17,1},{25,9},{2,18},{10... | collective-permute-start | bytes 1769480 | tf_op jit(solution)/shard_map/ppermute | solution.py:1022
  77.8 15.8 %collective-permute-start.18 = (bf16[2,2,192,384]{3,2,1,0:T(8,128)(2,1)}, bf16[2,2,192,384]{3,2,1,0:T(8,128)(2,1)}, u32[]{:S(2)}, u32[]{:S(2)}) collective-permute-start(bf16[2,2,192,384]{3,2,1,0:T(8,128)(2,1)} %get-tuple-element.145), channel_id=1, source_target_pairs={{0,1},{1,0},{2,3},{3,2},{4,5},{5,4},{6,7},{7,6},{8,9},{9,8},{10,11... | collective-permute-start | bytes 1769480 | tf_op jit(solution)/shard_map/ppermute | solution.py:1022
  87.6 11.6 %copy-start.2 = (bf16[512,3840]{1,0:T(8,128)(2,1)S(1)}, bf16[512,3840]{1,0:T(8,128)(2,1)}, u32[]{:S(2)}) copy-start(bf16[512,3840]{1,0:T(8,128)(2,1)} %get-tuple-element.142.refs_2_) | copy-start | bytes 11796484
  88.8 16.5 %collective-permute-start.14 = (bf16[132,8,192]{2,1,0:T(8,128)(2,1)S(1)}, bf16[132,8,192]{2,1,0:T(8,128)(2,1)S(1)}, u32[]{:S(2)}, u32[]{:S(2)}) collective-permute-start(bf16[132,8,192]{2,1,0:T(8,128)(2,1)S(1)} %get-tuple-element.140.refs_4_), channel_id=1, source_target_pairs={{0,8},{8,0},{16,24},{24,16},{1,9},{9,1},{17,25},{25,17},{2,10},{10... | collective-permute-start | bytes 1216520 | tf_op jit(solution)/shard_map/ppermute | solution.py:1022
  95.1 10.3 %collective-permute-start.20 = (bf16[2,192,384]{2,1,0:T(8,128)(2,1)S(1)}, bf16[2,192,384]{2,1,0:T(8,128)(2,1)S(1)}, u32[]{:S(2)}, u32[]{:S(2)}) collective-permute-start(bf16[2,192,384]{2,1,0:T(8,128)(2,1)S(1)} %get-tuple-element.148), channel_id=1, source_target_pairs={{0,16},{8,24},{16,0},{24,8},{1,17},{9,25},{17,1},{25,9},{2,18},{10... | collective-permute-start | bytes 884744 | tf_op jit(solution)/shard_map/ppermute | solution.py:1022
  96.6 8.8 %collective-permute-start.19 = (bf16[2,192,384]{2,1,0:T(8,128)(2,1)S(1)}, bf16[2,192,384]{2,1,0:T(8,128)(2,1)S(1)}, u32[]{:S(2)}, u32[]{:S(2)}) collective-permute-start(bf16[2,192,384]{2,1,0:T(8,128)(2,1)S(1)} %get-tuple-element.146.refs_4_), channel_id=1, source_target_pairs={{0,1},{1,0},{2,3},{3,2},{4,5},{5,4},{6,7},{7,6},{8,9},{9,8},{10,11... | collective-permute-start | bytes 884744 | tf_op jit(solution)/shard_map/ppermute | solution.py:1022
  97.2 8.2 %collective-permute-start.15 = (bf16[64,1152]{1,0:T(8,128)(2,1)S(1)}, bf16[64,1152]{1,0:T(8,128)(2,1)S(1)}, u32[]{:S(2)}, u32[]{:S(2)}) collective-permute-start(bf16[64,1152]{1,0:T(8,128)(2,1)S(1)} %get-tuple-element.141.refs_3_), channel_id=1, source_target_pairs={{0,4},{1,5},{2,6},{3,7},{4,0},{5,1},{6,2},{7,3},{8,12},{9,13},{10,... | collective-permute-start | bytes 442376 | tf_op jit(solution)/shard_map/ppermute | solution.py:1022
  99.2 11.2 %collective-permute-start.22 = (bf16[528,2304]{1,0:T(8,128)(2,1)}, bf16[528,2304]{1,0:T(8,128)(2,1)}, u32[]{:S(2)}, u32[]{:S(2)}) collective-permute-start(bf16[528,2304]{1,0:T(8,128)(2,1)} %attention_back.1.rest_0_.refs_4_), channel_id=1, source_target_pairs={{0,8},{8,0},{16,24},{24,16},{1,9},{9,1},{17,25},{25,17},{2,10},{10... | collective-permute-start | bytes 7299080 | tf_op jit(solution)/shard_map/ppermute | solution.py:1022
  107.6 2.8 %copy-start.5 = (bf16[128,1152]{1,0:T(8,128)(2,1)}, bf16[128,1152]{1,0:T(8,128)(2,1)S(1)}, u32[]{:S(2)}) copy-start(bf16[128,1152]{1,0:T(8,128)(2,1)S(1)} %get-tuple-element.153.refs_4_.refs_0_) | copy-start | bytes 884740
  107.7 18.2 %collective-permute-start.21 = (bf16[960,384]{1,0:T(8,128)(2,1)S(1)}, bf16[960,384]{1,0:T(8,128)(2,1)S(1)}, u32[]{:S(2)}, u32[]{:S(2)}) collective-permute-start(bf16[960,384]{1,0:T(8,128)(2,1)S(1)} %get-tuple-element.150), channel_id=1, source_target_pairs={{0,1},{1,0},{2,3},{3,2},{4,5},{5,4},{6,7},{7,6},{8,9},{9,8},{10,11... | collective-permute-start | bytes 2211848 | tf_op jit(solution)/shard_map/ppermute | solution.py:1022
  108.9 28.9 %collective-permute-start.25 = (bf16[2,4,192,384]{3,2,1,0:T(8,128)(2,1)S(1)}, bf16[2,4,192,384]{3,2,1,0:T(8,128)(2,1)S(1)}, u32[]{:S(2)}, u32[]{:S(2)}) collective-permute-start(bf16[2,4,192,384]{3,2,1,0:T(8,128)(2,1)S(1)} %get-tuple-element.159), channel_id=1, source_target_pairs={{0,16},{8,24},{16,0},{24,8},{1,17},{9,25},{17,1},{25,9},{2,18},{10... | collective-permute-start | bytes 3538952 | tf_op jit(solution)/shard_map/ppermute | solution.py:1022
  110.4 18.3 %collective-permute-start.24 = (bf16[768,384]{1,0:T(8,128)(2,1)S(1)}, bf16[768,384]{1,0:T(8,128)(2,1)S(1)}, u32[]{:S(2)}, u32[]{:S(2)}) collective-permute-start(bf16[768,384]{1,0:T(8,128)(2,1)S(1)} %get-tuple-element.154.refs_6_), channel_id=1, source_target_pairs={{0,2},{1,3},{2,0},{3,1},{4,6},{5,7},{6,4},{7,5},{8,10},{9,11},{10,... | collective-permute-start | bytes 1769480 | tf_op jit(solution)/shard_map/ppermute | solution.py:1022
  110.5 1.8 copy-start.1
  112.2 2.1 %copy-start.3 = (bf16[512,3840]{1,0:T(8,128)(2,1)S(1)}, bf16[512,3840]{1,0:T(8,128)(2,1)}, u32[]{:S(2)}) copy-start(bf16[512,3840]{1,0:T(8,128)(2,1)} %get-tuple-element.142.refs_2_) | copy-start | bytes 11796484
  126.0 13.7 %collective-permute-start.23 = (bf16[576,384]{1,0:T(8,128)(2,1)S(1)}, bf16[576,384]{1,0:T(8,128)(2,1)S(1)}, u32[]{:S(2)}, u32[]{:S(2)}) collective-permute-start(bf16[576,384]{1,0:T(8,128)(2,1)S(1)} %get-tuple-element.157.refs_2_), channel_id=1, source_target_pairs={{0,2},{1,3},{2,0},{3,1},{4,6},{5,7},{6,4},{7,5},{8,10},{9,11},{10,... | collective-permute-start | bytes 1327112 | tf_op jit(solution)/shard_map/ppermute | solution.py:1022
  126.0 23.9 %collective-permute-start.28 = (bf16[2,2,208,384]{3,2,1,0:T(8,128)(2,1)}, bf16[2,2,208,384]{3,2,1,0:T(8,128)(2,1)}, u32[]{:S(2)}, u32[]{:S(2)}) collective-permute-start(bf16[2,2,208,384]{3,2,1,0:T(8,128)(2,1)} %get-tuple-element.168), channel_id=1, source_target_pairs={{0,16},{8,24},{16,0},{24,8},{1,17},{9,25},{17,1},{25,9},{2,18},{10... | collective-permute-start | bytes 1916936 | tf_op jit(solution)/shard_map/ppermute | solution.py:1022
  127.0 23.0 %collective-permute-start.29 = (bf16[2,2,208,384]{3,2,1,0:T(8,128)(2,1)}, bf16[2,2,208,384]{3,2,1,0:T(8,128)(2,1)}, u32[]{:S(2)}, u32[]{:S(2)}) collective-permute-start(bf16[2,2,208,384]{3,2,1,0:T(8,128)(2,1)} %get-tuple-element.170), channel_id=1, source_target_pairs={{0,1},{1,0},{2,3},{3,2},{4,5},{5,4},{6,7},{7,6},{8,9},{9,8},{10,11... | collective-permute-start | bytes 1916936 | tf_op jit(solution)/shard_map/ppermute | solution.py:1022
  138.8 2.9 %copy-start.9 = (s32[2,4]{1,0:T(2,128)S(1)}, s32[2,4]{1,0:T(2,128)}, u32[]{:S(2)}) copy-start(s32[2,4]{1,0:T(2,128)} %len_ref.3) | copy-start | bytes 100
  138.8 23.6 %collective-permute-start.27 = (bf16[4,192,384]{2,1,0:T(8,128)(2,1)}, bf16[4,192,384]{2,1,0:T(8,128)(2,1)}, u32[]{:S(2)}, u32[]{:S(2)}) collective-permute-start(bf16[4,192,384]{2,1,0:T(8,128)(2,1)} %get-tuple-element.160.rest_0_), channel_id=1, source_target_pairs={{0,1},{1,0},{2,3},{3,2},{4,5},{5,4},{6,7},{7,6},{8,9},{9,8},{10,11... | collective-permute-start | bytes 1769480 | tf_op jit(solution)/shard_map/ppermute | solution.py:1022
  140.5 21.9 %collective-permute-start.26 = (bf16[576,384]{1,0:T(8,128)(2,1)}, bf16[576,384]{1,0:T(8,128)(2,1)}, u32[]{:S(2)}, u32[]{:S(2)}) collective-permute-start(bf16[576,384]{1,0:T(8,128)(2,1)} %get-tuple-element.166), channel_id=1, source_target_pairs={{0,4},{1,5},{2,6},{3,7},{4,0},{5,1},{6,2},{7,3},{8,12},{9,13},{10,... | collective-permute-start | bytes 1327112 | tf_op jit(solution)/shard_map/ppermute | solution.py:1022
  150.0 1.4 copy-start.4
  153.0 25.5 %copy-start.6 = (bf16[128,1152]{1,0:T(8,128)(2,1)S(1)}, bf16[128,1152]{1,0:T(8,128)(2,1)}, u32[]{:S(2)}) copy-start(bf16[128,1152]{1,0:T(8,128)(2,1)} %copy-done.5) | copy-start | bytes 884740
  153.0 8.0 %collective-permute-start.31 = (bf16[2,208,384]{2,1,0:T(8,128)(2,1)S(1)}, bf16[2,208,384]{2,1,0:T(8,128)(2,1)S(1)}, u32[]{:S(2)}, u32[]{:S(2)}) collective-permute-start(bf16[2,208,384]{2,1,0:T(8,128)(2,1)S(1)} %get-tuple-element.174), channel_id=1, source_target_pairs={{0,16},{8,24},{16,0},{24,8},{1,17},{9,25},{17,1},{25,9},{2,18},{10... | collective-permute-start | bytes 958472 | tf_op jit(solution)/shard_map/ppermute | solution.py:1022
  154.5 8.0 %collective-permute-start.30 = (bf16[2,208,384]{2,1,0:T(8,128)(2,1)S(1)}, bf16[2,208,384]{2,1,0:T(8,128)(2,1)S(1)}, u32[]{:S(2)}, u32[]{:S(2)}) collective-permute-start(bf16[2,208,384]{2,1,0:T(8,128)(2,1)S(1)} %get-tuple-element.172.refs_6_), channel_id=1, source_target_pairs={{0,1},{1,0},{2,3},{3,2},{4,5},{5,4},{6,7},{7,6},{8,9},{9,8},{10,11... | collective-permute-start | bytes 958472 | tf_op jit(solution)/shard_map/ppermute | solution.py:1022
  164.2 13.5 %collective-permute-start.33 = (bf16[2,208,384]{2,1,0:T(8,128)(2,1)S(1)}, bf16[2,208,384]{2,1,0:T(8,128)(2,1)S(1)}, u32[]{:S(2)}, u32[]{:S(2)}) collective-permute-start(bf16[2,208,384]{2,1,0:T(8,128)(2,1)S(1)} %get-tuple-element.178), channel_id=1, source_target_pairs={{0,2},{1,3},{2,0},{3,1},{4,6},{5,7},{6,4},{7,5},{8,10},{9,11},{10,... | collective-permute-start | bytes 958472 | tf_op jit(solution)/shard_map/ppermute | solution.py:1022
  165.2 12.4 %collective-permute-start.32 = (bf16[2,192,384]{2,1,0:T(8,128)(2,1)S(1)}, bf16[2,192,384]{2,1,0:T(8,128)(2,1)S(1)}, u32[]{:S(2)}, u32[]{:S(2)}) collective-permute-start(bf16[2,192,384]{2,1,0:T(8,128)(2,1)S(1)} %get-tuple-element.176.rest_0_), channel_id=1, source_target_pairs={{0,2},{1,3},{2,0},{3,1},{4,6},{5,7},{6,4},{7,5},{8,10},{9,11},{10,... | collective-permute-start | bytes 884744 | tf_op jit(solution)/shard_map/ppermute | solution.py:1022
  177.8 13.3 %collective-permute-start.34 = (bf16[400,384]{1,0:T(8,128)(2,1)S(1)}, bf16[400,384]{1,0:T(8,128)(2,1)S(1)}, u32[]{:S(2)}, u32[]{:S(2)}) collective-permute-start(bf16[400,384]{1,0:T(8,128)(2,1)S(1)} %get-tuple-element.180.refs_4_), channel_id=1, source_target_pairs={{0,4},{1,5},{2,6},{3,7},{4,0},{5,1},{6,2},{7,3},{8,12},{9,13},{10,... | collective-permute-start | bytes 921608 | tf_op jit(solution)/shard_map/ppermute | solution.py:1022
  (1 other events, 0.7 us)
